TPU v7x, 256 devices: a whole 4x4x8 slice. The times are simulated.
256 devices in a mesh: dp: 64 (over x, z, core), section: 4 (over y).
Axes of the slice: x: 4, y: 4, z: 8, core: 2. Of those that a mesh axis runs over, the one named last changes fastest.
Arguments:
- acts: bfloat16 [4, 49152, 4608], P('section', 'dp'), may hold values from -16 to 16
- grad_out: bfloat16 [4, 49152, 512], P('section', 'dp'), may hold values from -0.02734375 to 0.02734375
- params: float32 [4, 18432, 128], P('section', 'dp'), may hold values from -0.3125 to 0.3125
- moment1: float32 [4, 18432, 128], P('section', 'dp'), may hold values from -4 to 4
- moment2: float32 [4, 18432, 128], P('section', 'dp'), may hold values from 0.01 to 0.1
- ema: float32 [4, 18432, 128], P('section', 'dp'), may hold values from -0.3125 to 0.3125
- live_rows: int32 [4], replicated, may hold values from 9216 to 18432
- home: int32 [4, 9], replicated, may hold values from 0 to 3, as said below
Outputs:
- new_params: float32 [4, 18432, 128], P('section', 'dp')
- new_moment1: float32 [4, 18432, 128], P('section', 'dp')
- new_moment2: float32 [4, 18432, 128], P('section', 'dp')
- new_ema: float32 [4, 18432, 128], P('section', 'dp')
- weights: bfloat16 [4, 4608, 512], P('section')
Inputs may be any that keep to these rules, and one draw needn't show every extreme that they name: Every section is home of exactly 9 blocks.
All inputs are finite; a program needn't handle non-finite values.
Results may differ from a plain program's by a relative error of at most 0.0075.
Values may be sent and summed in bfloat16 or wider, within the bound.
A program may use at most 128 MiB of HBM per device.

v0:
```python
import jax
import jax.numpy as jnp
from jax import lax
from jax.sharding import PartitionSpec as P

N_GEN = 2
STEP = 100


def home_tables(home, nblk):
    flat = home.reshape(-1)
    total = flat.shape[0]
    counter = jnp.arange(total, dtype=jnp.int32)
    earlier = (flat[None, :] == flat[:, None]) & (counter[None, :] < counter[:, None])
    ranks = jnp.sum(earlier.astype(jnp.int32), axis=1)
    position = flat * nblk + ranks
    order = jnp.sum(jnp.where(position[None, :] == counter[:, None], counter[None, :], 0), axis=1)
    return (position, order)


def adam_update(params, moment1, moment2, ema, grads, alive, generator):
    corr_one = 1.0 - 0.9**STEP
    corr_two = 1.0 - 0.99**STEP
    first = jnp.where(alive, 0.9 * moment1 + 0.1 * grads, moment1)
    second = jnp.where(alive, 0.99 * moment2 + 0.01 * grads * grads, moment2)
    stepped = params - 0.0025 * (first / corr_one) / (jnp.sqrt(second / corr_two) + 1e-08)
    updated = jnp.where(alive, stepped, params)
    averaged = jnp.where(generator, 0.995 * ema + 0.005 * updated, ema)
    return (updated, first, second, averaged)


def body(acts, grad_out, params, moment1, moment2, ema, live_rows, home):
    inputs_here = acts[0]
    cotangent = grad_out[0]
    channels = cotangent.shape[1]
    shard_rows = params.shape[1]
    blocks = home.shape[1]
    block_rows = shard_rows // blocks
    sections = lax.axis_size("section")
    product = lax.dot_general(
        inputs_here, cotangent, (((0,), (0,)), ((), ())), preferred_element_type=jnp.float32
    )
    summed = lax.psum_scatter(
        product.reshape(lax.axis_size("dp") * shard_rows, 128),
        "dp",
        scatter_dimension=0,
        tiled=True,
    )
    position, order = home_tables(home, blocks)
    section_here = lax.axis_index("section")
    dp_here = lax.axis_index("dp")
    owned = lax.dynamic_slice_in_dim(order, section_here * blocks, blocks)
    everyone = lax.all_gather(
        summed[None].astype(jnp.bfloat16), "section", axis=0, tiled=True
    ).astype(jnp.float32)
    grads = everyone.reshape(sections * blocks, block_rows, 128)[owned].reshape(shard_rows, 128)
    source = owned // blocks
    within = owned % blocks
    section_ids = jnp.arange(sections, dtype=jnp.int32)
    limits = jnp.sum(
        jnp.where(source[:, None] == section_ids[None, :], live_rows[None, :], 0), axis=1
    )
    global_row = (
        dp_here * shard_rows
        + within[:, None] * block_rows
        + jnp.arange(block_rows, dtype=jnp.int32)[None, :]
    )
    alive = (global_row < limits[:, None]).reshape(shard_rows, 1)
    generator = jnp.broadcast_to((source < N_GEN)[:, None], (blocks, block_rows)).reshape(
        shard_rows, 1
    )
    updated, first, second, averaged = adam_update(
        params[0], moment1[0], moment2[0], ema[0], grads, alive, generator
    )
    rounded = updated.astype(jnp.bfloat16)
    collected = lax.all_gather(rounded[None], ("dp", "section"), axis=0, tiled=True)
    dp_count = collected.shape[0] // sections
    collected = collected.reshape(dp_count, sections * blocks, block_rows, 128)
    wanted = lax.dynamic_slice_in_dim(position, section_here * blocks, blocks)
    weights = collected[:, wanted].reshape(-1, channels)
    return (updated[None], first[None], second[None], averaged[None], weights[None])


def solution(mesh):
    in_specs = (
        P("section", "dp", None),
        P("section", "dp", None),
        P("section", "dp", None),
        P("section", "dp", None),
        P("section", "dp", None),
        P("section", "dp", None),
        P(),
        P(),
    )
    out_specs = (
        P("section", "dp", None),
        P("section", "dp", None),
        P("section", "dp", None),
        P("section", "dp", None),
        P("section", None, None),
    )
    return jax.shard_map(body, mesh=mesh, in_specs=in_specs, out_specs=out_specs, check_vma=False)
```

profile of v0, /device:TPU:1, one launch (start us, length us, event | category | flops | bytes accessed | tf_op | source)
XLA Modules:
  0.0 358.5 jit_solution(15467340698909036543)
XLA Ops:
  7.2 0.0 copy-start
  7.2 0.0 reduce-scatter.2.cloned.1.call-start
  7.2 1.1 copy-done
  8.3 9.3 %fusion = f32[4608,512]{1,0:T(8,128)} fusion(bf16[1,768,4608]{2,1,0:T(8,128)(2,1)} %param.8, bf16[1,768,512]{2,1,0:T(8,128)(2,1)S(1)} %copy-done), kind=kOutput, calls=%fused_computation.2 | convolution fusion | flops 3623878656 | bytes 17301504 | tf_op jit(solution)/shard_map/dot_general | solution.py:40
  17.6 10.8 %reshape.188 = f32[18432,128]{1,0:T(8,128)} reshape(f32[4608,512]{1,0:T(8,128)} %fusion) | data formatting | bytes 18874368 | tf_op jit(solution)/shard_map/reshape | solution.py:44
  28.4 0.0 copy-start.6
  28.4 0.0 copy-start.7
  28.4 0.0 copy-start.2
  28.4 0.0 copy-start.3
  28.4 0.0 copy-start.4
  28.4 0.0 copy-start.5
  28.4 0.0 reduce-scatter.2.cloned.1.call-update
  28.5 0.0 all-gather.3.cloned.1.call-start
  28.5 0.6 copy-done.6
  29.1 0.1 reshape.187
  29.2 0.2 convert_reduce_fusion
  29.4 0.1 select_reduce_fusion
  29.5 0.1 broadcast_compare_fusion
  29.6 0.1 compare_select_fusion.1
  29.7 0.0 copy-done.7
  29.7 0.1 select_reduce_fusion.1
  29.8 0.1 add_compare_fusion
  29.8 0.1 lt.60
  29.9 152.1 %reduce-scatter.2.cloned.1.call-done = f32[288,128]{1,0:T(8,128)} async-done(((f32[18432,128]{1,0:T(8,128)}), f32[288,128]{1,0:T(8,128)}) %reduce-scatter.2.cloned.1.call-update) | async-done | bytes 147472 | tf_op jit(solution)/shard_map/reduce_scatter | solution.py:43
  182.1 0.9 convert_element_type.15
  183.0 10.1 %all-gather = bf16[1152,128]{1,0:T(8,128)(2,1)S(1)} all-gather(bf16[288,128]{1,0:T(8,128)(2,1)S(1)} %convert_element_type.15), channel_id=2, replica_groups=mesh['dp'=64,'section'=4] {'section'}, dimensions={0}, use_global_device_ids=true | all-gather | bytes 368640 | tf_op jit(solution)/shard_map/all_gather | solution.py:53
  193.1 0.1 convert.1
  193.2 0.6 gather_fusion
  193.7 0.0 copy-done.2
  193.8 0.0 copy-done.3
  193.8 0.0 copy-done.4
  193.8 0.9 fusion.10
  194.7 0.0 copy-start.1
  194.7 0.0 all-gather.3.cloned.1.call-update
  194.7 0.1 broadcast_in_dim.77
  194.8 0.1 broadcast_in_dim.78
  194.9 0.1 compare_select_fusion
  194.9 0.0 copy-done.5
  194.9 0.8 add_select_fusion
  195.7 132.1 %all-gather.3.cloned.1.call-done = bf16[256,288,128]{2,1,0:T(8,128)(2,1)} async-done(((bf16[1,288,128]{2,1,0:T(8,128)(2,1)}), bf16[256,288,128]{2,1,0:T(8,128)(2,1)}) %all-gather.3.cloned.1.call-update) | async-done | bytes 18874384 | tf_op jit(solution)/shard_map/all_gather | solution.py:76
  327.8 10.1 %gather_fusion.1 = bf16[9,64,32,128]{3,2,1,0:T(8,128)(2,1)} fusion(bf16[64,36,32,128]{3,2,1,0:T(8,128)(2,1)} %bitcast.23, s32[1024]{0:T(1024)S(1)} %pad_clamp_fusion), kind=kCustom, calls=%fused_computation.1 | custom fusion | bytes 9437220 | tf_op jit(solution)/shard_map/gather | solution.py:80
  337.9 5.3 %copy.15 = bf16[64,9,32,128]{3,2,1,0:T(8,128)(2,1)} copy(bf16[64,9,32,128]{3,2,0,1:T(8,128)(2,1)} %bitcast.21) | data formatting | bytes 9437184 | tf_op jit(solution)/shard_map/gather | solution.py:80
  343.2 0.0 copy-done.1
  343.2 8.5 %broadcast_in_dim_reshape.2 = bf16[1,4608,512]{2,1,0:T(8,128)(2,1)} reshape(bf16[64,9,32,128]{3,2,1,0:T(8,128)(2,1)} %copy.15) | data formatting | bytes 9437184 | tf_op jit(solution)/shard_map/broadcast_in_dim;reshape | solution.py:81
  (3 shorter events, 0.0 us)
Async XLA Ops:
  7.2 1.1 copy-start
  7.2 174.9 %reduce-scatter.2.cloned.1.call-start = ((), (), s32[]{:S(2)}) async-start(), calls=%async_computation.1 | async-start | bytes 9584640 | tf_op jit(solution)/shard_map/reduce_scatter | solution.py:43
  28.4 0.7 copy-start.6
  28.4 1.3 copy-start.7
  28.4 165.3 %copy-start.2 = (f32[1,288,128]{2,1,0:T(8,128)S(1)}, f32[1,288,128]{2,1,0:T(8,128)}, u32[]{:S(2)}) copy-start(f32[1,288,128]{2,1,0:T(8,128)} %param.10) | copy-start | bytes 442372
  28.4 165.3 %copy-start.3 = (f32[1,288,128]{2,1,0:T(8,128)S(1)}, f32[1,288,128]{2,1,0:T(8,128)}, u32[]{:S(2)}) copy-start(f32[1,288,128]{2,1,0:T(8,128)} %param.11) | copy-start | bytes 442372
  28.4 165.3 %copy-start.4 = (f32[1,288,128]{2,1,0:T(8,128)S(1)}, f32[1,288,128]{2,1,0:T(8,128)}, u32[]{:S(2)}) copy-start(f32[1,288,128]{2,1,0:T(8,128)} %param.12) | copy-start | bytes 442372
  28.4 166.5 %copy-start.5 = (f32[1,288,128]{2,1,0:T(8,128)S(1)}, f32[1,288,128]{2,1,0:T(8,128)}, u32[]{:S(2)}) copy-start(f32[1,288,128]{2,1,0:T(8,128)} %param.13) | copy-start | bytes 442372
  28.5 299.3 %all-gather.3.cloned.1.call-start = ((), (), s32[]{:S(2)}) async-start(), calls=%async_computation.2 | async-start | bytes 18948096 | tf_op jit(solution)/shard_map/all_gather | solution.py:76
  194.7 148.5 %copy-start.1 = (f32[1,288,128]{2,1,0:T(8,128)}, f32[1,288,128]{2,1,0:T(8,128)S(1)}, u32[]{:S(2)}) copy-start(f32[1,288,128]{2,1,0:T(8,128)S(1)} %get-tuple-element.6) | copy-start | bytes 442372
Sparse Core Ops, SparseCore 0:
  28.6 153.4 reduce-scatter.1
  194.8 132.9 all-gather.2
where the time goes:
time: 359 us
  waiting for transfers between devices  284 us (79%)
  local copies, waits for them, and re-layouts  37.2 us (10%)
  between operations  14.1 us (4%)
  blocking collectives  10.1 us (3%)
  matrix products  9.33 us (3%)
    reduce_scatter x1, waiting for transfers between devices, body(): lax.psum_scatter(product.reshape(lax.axis_size('dp') * shard_rows, 128),...  152 us
    all_gather x1, waiting for transfers between devices, body(): lax.all_gather(rounded[None], ('dp', 'section'), axis=0, tiled=True)  132 us
    gather x2, local copies, waits for them, and re-layouts, body(): weights = collected[:, wanted].reshape(-1, channels)  15.4 us
    reshape x1, local copies, waits for them, and re-layouts, body(): product.reshape(lax.axis_size('dp') * shard_rows, 128)  10.8 us
    all_gather x1, blocking collectives, body(): lax.all_gather(summed[None].astype(jnp.bfloat16), 'section', axis=0, tile...  10.1 us
    dot_general x1, matrix products, body(): lax.dot_general(inputs_here, cotangent, (((0,), (0,)), ((), ())), preferr...  9.33 us
    another operation x1, local copies, waits for them, and re-layouts, body(): weights[None]  8.49 us
  transfers between devices with their start and end apart: 2, of which 2 were waited for; matrix products, arithmetic and copies ran while one was open for 1% of the time, Pallas kernels for 0%

commit v1 on v0

v1 whole, which is shorter than its diff:
```python
import jax
import jax.numpy as jnp
from jax import lax
from jax.experimental import pallas as pl
from jax.experimental.pallas import tpu as pltpu
from jax.sharding import PartitionSpec as P

N_GEN = 2
STEP = 100
MESH = pl.DeviceIdType.MESH
BF16, F32 = jnp.bfloat16, jnp.float32

X, Z, Y = 4, 8, 4
LANES = 128
HALF = 72
PIECE = 2 * HALF
BLOCKS = 9
OFFSETS = (2, 1, 3, 0)

S_CORE = 0
S_A1 = S_CORE + 4
S_B1 = S_A1 + 3
S_A2 = S_B1 + 7
S_B2 = S_A2 + 7
S_G = S_B2 + 3
S_H = S_G + 7
S_WA1 = S_H + 7
S_WB1 = S_WA1 + 7
S_WA2 = S_WB1 + 3
S_WB2 = S_WA2 + 3
S_WC = S_WB2 + 7
N_REMOTE = S_WC + 12

L_ACTS = 0
L_COT = L_ACTS + 4
L_STATE = L_COT + 2
L_NEW = L_STATE + 4
L_OUT = L_NEW + 4
N_LOCAL = L_OUT + 24


def kernel(
    acts, cot, params, moment1, moment2, ema, live_rows, home,
    new_params, new_moment1, new_moment2, new_ema, weights,
    acts_buf, cot_buf, own, core_out, core_in,
    a1_out, a1_in, b1_out, b1_in, acc_a, acc_b, a2_out, a2_in, b2_out, b2_in,
    g_out, g_in, g_all, state, fresh, h_all, h_out, h_in, w_all, w_mine, gathered,
    position, order, send_sems, recv_sems, local_sems,
):
    dp = lax.axis_index("dp")
    y = lax.axis_index("section")
    c = lax.rem(dp, 2)
    z = lax.rem(lax.div(dp, 2), Z)
    x = lax.div(dp, 2 * Z)
    sign = 1 - 2 * c

    def xi(k):
        return lax.rem(x + sign * k + 2 * X, X)

    def zi(k):
        return lax.rem(z + sign * k + 2 * Z, Z)

    def at(xx, zz, cc, yy):
        return ((xx * Z + zz) * 2 + cc, yy)

    x_next, x_last = at(xi(1), z, c, y), at(xi(-1), z, c, y)
    z_next, z_last = at(x, zi(1), c, y), at(x, zi(-1), c, y)
    partner = at(x, z, 1 - c, y)
    others = []
    for dy in range(Y):
        for dc in range(2):
            if dy or dc:
                others.append((lax.rem(c + dc, 2), lax.rem(y + dy, Y)))

    barrier = pltpu.get_barrier_semaphore()
    greeted = [x_next, x_last, z_next, z_last] + [at(x, z, cc, yy) for cc, yy in others]
    for device in greeted:
        pl.semaphore_signal(barrier, inc=1, device_id=device, device_id_type=MESH)

    pending = []

    def local(src, dst, index):
        copy = pltpu.make_async_copy(src, dst, local_sems.at[index])
        copy.start()
        return copy

    def send(src, dst, device, index):
        copy = pltpu.make_async_remote_copy(
            src_ref=src, dst_ref=dst, send_sem=send_sems.at[index], recv_sem=recv_sems.at[index],
            device_id=device, device_id_type=MESH,
        )
        copy.start()
        pending.append(copy)
        return copy

    width = Z * PIECE
    cot_copies = []
    for half in range(2):
        column = pl.multiple_of(256 * lax.rem(c + half, 2), 256)
        cot_copies.append(
            local(cot.at[:, pl.ds(column, 256)], cot_buf.at[:, pl.ds(256 * half, 256)], L_COT + half)
        )
    for t, offset in enumerate(OFFSETS):
        column = pl.multiple_of(width * lax.rem(x + offset, X), LANES)
        local(acts.at[:, pl.ds(column, width)], acts_buf.at[t], L_ACTS + t)
    state_copies = [
        local(ref, state.at[n], L_STATE + n) for n, ref in enumerate((params, moment1, moment2, ema))
    ]

    def section_row(s, carry):
        def block_entry(b, carry):
            counts, kept = carry[:Y], carry[Y:]
            keeper = home[s, b]
            rank = jnp.int32(0)
            for n in range(Y):
                rank = jnp.where(keeper == n, counts[n], rank)
            place = keeper * BLOCKS + rank
            position[s * BLOCKS + b] = place
            counts = tuple(counts[n] + jnp.where(keeper == n, 1, 0) for n in range(Y))
            here = place - y * BLOCKS
            kept = tuple(jnp.where(here == n, s * BLOCKS + b, kept[n]) for n in range(BLOCKS))
            return counts + kept

        return lax.fori_loop(0, BLOCKS, block_entry, carry)

    table = lax.fori_loop(0, Y, section_row, (jnp.int32(0),) * (Y + BLOCKS))
    for n in range(BLOCKS):
        order[n] = table[Y + n]

    pl.semaphore_wait(barrier, len(greeted))

    for copy in cot_copies:
        copy.wait()

    def core_copy(t):
        return pltpu.make_async_remote_copy(
            src_ref=core_out.at[t], dst_ref=core_in.at[t],
            send_sem=send_sems.at[S_CORE + t], recv_sem=recv_sems.at[S_CORE + t],
            device_id=partner, device_id_type=MESH,
        )

    @pl.loop(0, X)
    def _(t):
        pltpu.make_async_copy(
            acts.at[:, pl.ds(0, width)], acts_buf.at[t], local_sems.at[L_ACTS + t]
        ).wait()
        product = lax.dot_general(
            acts_buf[t], cot_buf[...], (((0,), (0,)), ((), ())), preferred_element_type=F32
        )
        for h in range(2):
            own[t, h] = product[:, LANES * h : LANES * (h + 1)].reshape(Z, PIECE, LANES)
            other = product[:, 256 + LANES * h : 256 + LANES * (h + 1)]
            core_out[t, h] = other.reshape(Z, PIECE, LANES).astype(BF16)
        core_copy(t).start()

    pending += [core_copy(t) for t in range(X)]

    plus, minus = 1 + c, 2 - c

    def block_a(t):
        return own[t, 0] + core_in[t, 0].astype(F32)

    def block_b(zz):
        return own[:, 1, zz] + core_in[:, 1, zz].astype(F32)

    def give(value, out, into, slot, device, base):
        out[slot] = value.astype(BF16)
        return send(out.at[slot], into.at[slot], device, base + slot)

    def taken(copy, into, slot):
        copy.wait_recv()
        return into[slot].astype(F32)

    core_copy(0).wait_recv()
    a1, b1, a2, b2 = {}, {}, {}, {}
    a1[0] = give(block_a(0), a1_out, a1_in, 0, x_next, S_A1)
    for t in range(1, X):
        core_copy(t).wait_recv()
    b1[0] = give(block_b(zi(4)), b1_out, b1_in, 0, z_next, S_B1)
    b1[4] = give(block_b(zi(-3)), b1_out, b1_in, 4, z_last, S_B1)
    a1[2] = give(block_a(minus), a1_out, a1_in, 2, x_last, S_A1)
    b1[1] = give(block_b(zi(3)) + taken(b1[0], b1_in, 0), b1_out, b1_in, 1, z_next, S_B1)
    b1[5] = give(block_b(zi(-2)) + taken(b1[4], b1_in, 4), b1_out, b1_in, 5, z_last, S_B1)
    a1[1] = give(block_a(plus) + taken(a1[0], a1_in, 0), a1_out, a1_in, 1, x_next, S_A1)
    b1[2] = give(block_b(zi(2)) + taken(b1[1], b1_in, 1), b1_out, b1_in, 2, z_next, S_B1)
    b1[6] = give(block_b(zi(-1)) + taken(b1[5], b1_in, 5), b1_out, b1_in, 6, z_last, S_B1)
    b1[3] = give(block_b(zi(1)) + taken(b1[2], b1_in, 2), b1_out, b1_in, 3, z_next, S_B1)

    acc_a[...] = block_a(3) + taken(a1[2], a1_in, 2) + taken(a1[1], a1_in, 1)
    a2[0] = give(acc_a[zi(4)], a2_out, a2_in, 0, z_next, S_A2)
    a2[4] = give(acc_a[zi(-3)], a2_out, a2_in, 4, z_last, S_A2)
    acc_b[...] = block_b(z) + taken(b1[6], b1_in, 6) + taken(b1[3], b1_in, 3)
    b2[0] = give(acc_b[0], b2_out, b2_in, 0, x_next, S_B2)
    b2[2] = give(acc_b[minus], b2_out, b2_in, 2, x_last, S_B2)
    a2[1] = give(acc_a[zi(3)] + taken(a2[0], a2_in, 0), a2_out, a2_in, 1, z_next, S_A2)
    a2[5] = give(acc_a[zi(-2)] + taken(a2[4], a2_in, 4), a2_out, a2_in, 5, z_last, S_A2)
    b2[1] = give(acc_b[plus] + taken(b2[0], b2_in, 0), b2_out, b2_in, 1, x_next, S_B2)
    a2[2] = give(acc_a[zi(2)] + taken(a2[1], a2_in, 1), a2_out, a2_in, 2, z_next, S_A2)
    a2[6] = give(acc_a[zi(-1)] + taken(a2[5], a2_in, 5), a2_out, a2_in, 6, z_last, S_A2)
    a2[3] = give(acc_a[zi(1)] + taken(a2[2], a2_in, 2), a2_out, a2_in, 3, z_next, S_A2)
    sum_b = acc_b[3] + taken(b2[2], b2_in, 2) + taken(b2[1], b2_in, 1)
    sum_a = acc_a[z] + taken(a2[6], a2_in, 6) + taken(a2[3], a2_in, 3)

    mine = 2 * y + c

    def spread(out, into, base):
        into[mine] = out[c]
        copies = []
        for n, (cc, yy) in enumerate(others):
            copies.append(send(out.at[cc], into.at[mine], at(x, z, cc, yy), base + n))
        for copy in copies:
            copy.wait_recv()

    for cc in range(2):
        rows = slice(HALF * cc, HALF * (cc + 1))
        g_out[cc] = jnp.concatenate([sum_a[rows], sum_b[rows]], axis=0).astype(BF16)
    spread(g_out, g_in, S_G)
    for s in range(Y):
        for cc in range(2):
            value = g_in[2 * s + cc].astype(F32)
            for jj in range(2):
                g_all[2 * cc + jj, BLOCKS * s : BLOCKS * (s + 1)] = value[HALF * jj : HALF * (jj + 1)].reshape(
                    BLOCKS, 8, LANES
                )

    for copy in state_copies:
        copy.wait()
    corr_one = 1.0 - 0.9**STEP
    corr_two = 1.0 - 0.99**STEP

    @pl.loop(0, BLOCKS)
    def _(i):
        f = order[i]
        s = lax.div(f, BLOCKS)
        b = f - s * BLOCKS
        limit = live_rows[s] - (dp * (4 * HALF) + b * 32)
        tile = lax.broadcasted_iota(jnp.int32, (8, LANES), 0)
        generator = tile * 0 + s < N_GEN
        for j in range(4):
            rows = pl.ds(i * 32 + j, 8, stride=4)
            grads = g_all[j, f]
            alive = tile * 4 + j < limit
            p, m1, m2, average = (state[n, rows, :] for n in range(4))
            first = jnp.where(alive, 0.9 * m1 + 0.1 * grads, m1)
            second = jnp.where(alive, 0.99 * m2 + 0.01 * grads * grads, m2)
            stepped = p - 0.0025 * (first / corr_one) / (jnp.sqrt(second / corr_two) + 1e-08)
            updated = jnp.where(alive, stepped, p)
            averaged = jnp.where(generator, 0.995 * average + 0.005 * updated, average)
            for n, value in enumerate((updated, first, second, averaged)):
                fresh[n, rows, :] = value
            h_all[j, pl.ds(pl.multiple_of(i * 8, 8), 8), :] = updated

    for cc in range(2):
        h_out[cc] = h_all[2 * cc : 2 * cc + 2].reshape(PIECE, LANES).astype(BF16)
    spread(h_out, h_in, S_H)
    fresh_copies = [
        local(fresh.at[n], ref, L_NEW + n)
        for n, ref in enumerate((new_params, new_moment1, new_moment2, new_ema))
    ]
    for s in range(Y):
        for cc in range(2):
            value = h_in[2 * s + cc].astype(F32)
            for jj in range(2):
                w_all[jj, cc, BLOCKS * s : BLOCKS * (s + 1)] = value[HALF * jj : HALF * (jj + 1)].reshape(
                    BLOCKS, 8, LANES
                )

    @pl.loop(0, BLOCKS)
    def _(b):
        place = position[y * BLOCKS + b]
        for cc in range(2):
            for jj in range(2):
                w_mine[jj, pl.ds(pl.multiple_of(HALF * cc + b * 8, 8), 8), :] = w_all[jj, cc, place]

    ja, jb = 2 * c, 2 * c + 1
    gathered[ja, x, z] = w_mine[0].astype(BF16)
    gathered[jb, x, z] = w_mine[1].astype(BF16)
    finished = []

    def columns(j):
        return pl.ds(pl.multiple_of(j * LANES, LANES), LANES)

    def store_x(j, xx, index):
        finished.append(local(gathered.at[j, xx], weights.at[xx, :, :, columns(j)], L_OUT + index))

    def store_z(j, zz, index):
        finished.append(local(gathered.at[j, :, zz], weights.at[:, zz, :, columns(j)], L_OUT + index))

    crossing = {}

    def ready_x(xx, index):
        ref = gathered.at[ja, xx]
        crossing[index] = send(ref, ref, partner, S_WC + index)
        store_x(ja, xx, index)

    def ready_z(zz, index):
        ref = gathered.at[jb, :, zz]
        crossing[4 + index] = send(ref, ref, partner, S_WC + 4 + index)
        store_z(jb, zz, 4 + index)

    def pass_on(ref, device, index):
        return send(ref, ref, device, index)

    def chunk_a(k):
        return gathered.at[ja, x, zi(k)]

    def chunk_b(k):
        return gathered.at[jb, xi(k), z]

    def row_a(k):
        return gathered.at[ja, xi(k)]

    def row_b(k):
        return gathered.at[jb, :, zi(k)]

    wa1 = {0: pass_on(chunk_a(0), z_next, S_WA1), 4: pass_on(chunk_a(0), z_last, S_WA1 + 4)}
    wb1 = {0: pass_on(chunk_b(0), x_next, S_WB1), 2: pass_on(chunk_b(0), x_last, S_WB1 + 2)}
    wb1[0].wait_recv()
    wb1[1] = pass_on(chunk_b(-1), x_next, S_WB1 + 1)
    for k in range(1, 4):
        wa1[k - 1].wait_recv()
        wa1[k] = pass_on(chunk_a(-k), z_next, S_WA1 + k)
        if k < 3:
            wa1[k + 3].wait_recv()
            wa1[k + 4] = pass_on(chunk_a(k), z_last, S_WA1 + 4 + k)
    wb1[2].wait_recv()
    wb1[1].wait_recv()
    wb2 = {0: pass_on(row_b(0), z_next, S_WB2), 4: pass_on(row_b(0), z_last, S_WB2 + 4)}
    ready_z(z, 0)
    wa1[6].wait_recv()
    wa1[3].wait_recv()
    wa2 = {0: pass_on(row_a(0), x_next, S_WA2), 2: pass_on(row_a(0), x_last, S_WA2 + 2)}
    ready_x(x, 0)
    for k in range(1, 4):
        wb2[k - 1].wait_recv()
        wb2[k] = pass_on(row_b(-k), z_next, S_WB2 + k)
        ready_z(zi(-k), 2 * k - 1)
        wb2[k + 3].wait_recv()
        if k < 3:
            wb2[k + 4] = pass_on(row_b(k), z_last, S_WB2 + 4 + k)
        ready_z(zi(k), 2 * k)
        if k == 2:
            wa2[0].wait_recv()
            wa2[1] = pass_on(row_a(-1), x_next, S_WA2 + 1)
            ready_x(xi(-1), 1)
            wa2[2].wait_recv()
            ready_x(xi(1), 2)
    wb2[3].wait_recv()
    ready_z(zi(-4), 7)
    wa2[1].wait_recv()
    ready_x(xi(-2), 3)

    qa, qb = 2 * (1 - c), 2 * (1 - c) + 1
    crossing[4].wait_recv()
    store_z(qb, z, 16)
    crossing[0].wait_recv()
    store_x(qa, x, 12)
    for k in range(1, 4):
        crossing[4 + 2 * k - 1].wait_recv()
        store_z(qb, zi(k), 16 + 2 * k - 1)
        crossing[4 + 2 * k].wait_recv()
        store_z(qb, zi(-k), 16 + 2 * k)
        if k == 2:
            crossing[1].wait_recv()
            store_x(qa, xi(1), 13)
            crossing[2].wait_recv()
            store_x(qa, xi(-1), 14)
    crossing[11].wait_recv()
    store_z(qb, zi(4), 23)
    crossing[3].wait_recv()
    store_x(qa, xi(2), 15)

    for copy in fresh_copies + finished:
        copy.wait()
    for copy in pending:
        copy.wait_send()


def body(acts, grad_out, params, moment1, moment2, ema, live_rows, home):
    tokens = acts.shape[1]
    rows = (4 * HALF, LANES)
    any_space = pl.BlockSpec(memory_space=pl.ANY)
    smem = pl.BlockSpec(memory_space=pltpu.SMEM)
    plane = (Z, PIECE, LANES)
    column = (X, PIECE, LANES)
    chunk = (PIECE, LANES)
    outs = pl.pallas_call(
        kernel,
        out_shape=[jax.ShapeDtypeStruct(rows, F32)] * 4
        + [jax.ShapeDtypeStruct((X, Z, PIECE, 4 * LANES), BF16)],
        in_specs=[any_space] * 6 + [smem] * 2,
        out_specs=[any_space] * 5,
        scratch_shapes=[
            pltpu.VMEM((X, tokens, Z * PIECE), BF16),
            pltpu.VMEM((tokens, 4 * LANES), BF16),
            pltpu.VMEM((X, 2) + plane, F32),
            pltpu.VMEM((X, 2) + plane, BF16),
            pltpu.VMEM((X, 2) + plane, BF16),
            pltpu.VMEM((3,) + plane, BF16),
            pltpu.VMEM((3,) + plane, BF16),
            pltpu.VMEM((7,) + column, BF16),
            pltpu.VMEM((7,) + column, BF16),
            pltpu.VMEM(plane, F32),
            pltpu.VMEM(column, F32),
            pltpu.VMEM((7,) + chunk, BF16),
            pltpu.VMEM((7,) + chunk, BF16),
            pltpu.VMEM((3,) + chunk, BF16),
            pltpu.VMEM((3,) + chunk, BF16),
            pltpu.VMEM((2,) + chunk, BF16),
            pltpu.VMEM((2 * Y,) + chunk, BF16),
            pltpu.VMEM((4, Y * BLOCKS, 8, LANES), F32),
            pltpu.VMEM((4,) + rows, F32),
            pltpu.VMEM((4,) + rows, F32),
            pltpu.VMEM((4, HALF, LANES), F32),
            pltpu.VMEM((2,) + chunk, BF16),
            pltpu.VMEM((2 * Y,) + chunk, BF16),
            pltpu.VMEM((2, 2, Y * BLOCKS, 8, LANES), F32),
            pltpu.VMEM((2,) + chunk, F32),
            pltpu.VMEM((4, X) + plane, BF16),
            pltpu.SMEM((Y * BLOCKS,), jnp.int32),
            pltpu.SMEM((BLOCKS,), jnp.int32),
            pltpu.SemaphoreType.DMA((N_REMOTE,)),
            pltpu.SemaphoreType.DMA((N_REMOTE,)),
            pltpu.SemaphoreType.DMA((N_LOCAL,)),
        ],
        compiler_params=pltpu.CompilerParams(
            collective_id=0, has_side_effects=True, vmem_limit_bytes=56 * 2**20
        ),
    )(acts[0], grad_out[0], params[0], moment1[0], moment2[0], ema[0], live_rows, home)
    updated, first, second, averaged, weights = outs
    return (
        updated[None], first[None], second[None], averaged[None],
        weights.reshape(1, X * Z * PIECE, 4 * LANES),
    )


def solution(mesh):
    split = P("section", "dp", None)
    in_specs = (split,) * 6 + (P(), P())
    out_specs = (split,) * 4 + (P("section", None, None),)
    return jax.shard_map(body, mesh=mesh, in_specs=in_specs, out_specs=out_specs, check_vma=False)
```

time: 359 us -> 104 us (0.29)
  waiting for transfers between devices: 284 us -> 0 us
  Pallas kernels: 0 us -> 92.2 us
  local copies, waits for them, and re-layouts: 37.2 us -> 11.1 us
  between operations: 14.1 us -> 0.64 us
  blocking collectives: 10.1 us -> 0 us
  matrix products: 9.33 us -> 0 us
    reduce_scatter x1 -> x0, waiting for transfers between devices: 152 us -> none  [body(): lax.psum_scatter(product.reshape(lax.axis_size('dp') * shard_rows, 128),...]
    all_gather x1 -> x0, waiting for transfers between devices: 132 us -> none  [body(): lax.all_gather(rounded[None], ('dp', 'section'), axis=0, tiled=True)]
    pallas_call x0 -> x1, Pallas kernels: none -> 92.2 us  [body(): pl.pallas_call(kernel, out_shape=[jax.ShapeDtypeStruct(rows, F32)] * 4 +...]
    gather x3 -> x0, local copies, waits for them, and re-layouts: 15.9 us -> none  [the longest x2 15.4 us: body(): weights = collected[:, wanted].reshape(-1, channels)]
    reshape x2 -> x0, local copies, waits for them, and re-layouts: 10.9 us -> none  [the longest x1 10.8 us: body(): product.reshape(lax.axis_size('dp') * shard_rows, 128)]
    all_gather x1 -> x0, blocking collectives: 10.1 us -> none  [body(): lax.all_gather(summed[None].astype(jnp.bfloat16), 'section', axis=0, tile...]
    unnamed x16 -> x5, local copies, waits for them, and re-layouts: 1.68 us -> 11.1 us
    dot_general x1 -> x0, matrix products: 9.33 us -> none  [body(): lax.dot_general(inputs_here, cotangent, (((0,), (0,)), ((), ())), preferr...]
  transfers between devices with their start and end apart: 2 -> 0, of which waited for: 2 -> 0; matrix products, arithmetic and copies ran while one was open for 1% -> 0% of each run, Pallas kernels for 0% -> 0%
where the time goes in v1:
time: 104 us
  Pallas kernels  92.2 us (89%)
  local copies, waits for them, and re-layouts  11.1 us (11%)
    pallas_call x1, Pallas kernels, body(): pl.pallas_call(kernel, out_shape=[jax.ShapeDtypeStruct(rows, F32)] * 4 +...  92.2 us
    unnamed x5, local copies, waits for them, and re-layouts  11.1 us

profile of v1, /device:TPU:1, one launch (start us, length us, event | category | flops | bytes accessed | tf_op | source)
XLA Modules:
  0.0 104.0 jit_solution(3049272381333342398)
XLA Ops:
  0.6 92.2 %shard_map.119 = (f32[288,128]{1,0:T(8,128)}, f32[288,128]{1,0:T(8,128)}, f32[288,128]{1,0:T(8,128)}, f32[288,128]{1,0:T(8,128)}, bf16[4,8,144,512]{3,2,1,0:T(8,128)(2,1)}) custom-call(bf16[768,4608]{1,0:T(8,128)(2,1)} %bitcast.11, bf16[768,512]{1,0:T(8,128)(2,1)} %bitcast.13, f32[288,128]{1,0:T(8,128)} %bitcast.18, f32[288,128]{1,0:T(8,128)} %bitcast.19, ...), custom_call_target="tpu_custom_call" | custom-call | tf_op jit(solution)/shard_map/pallas_call | solution.py:387
  92.8 1.6 %copy.18 = f32[1,288,128]{2,1,0:T(8,128)} copy(f32[1,288,128]{2,1,0:T(8,128)} %bitcast.17) | data formatting | bytes 294912
  94.4 1.6 %copy.19 = f32[1,288,128]{2,1,0:T(8,128)} copy(f32[1,288,128]{2,1,0:T(8,128)} %bitcast.16) | data formatting | bytes 294912
  96.0 1.6 %copy.20 = f32[1,288,128]{2,1,0:T(8,128)} copy(f32[1,288,128]{2,1,0:T(8,128)} %bitcast.15) | data formatting | bytes 294912
  97.6 1.6 %copy.21 = f32[1,288,128]{2,1,0:T(8,128)} copy(f32[1,288,128]{2,1,0:T(8,128)} %bitcast.14) | data formatting | bytes 294912
  99.2 4.8 %copy.22 = bf16[1,4608,512]{2,1,0:T(8,128)(2,1)} copy(bf16[1,4608,512]{2,1,0:T(8,128)(2,1)} %bitcast.12) | data formatting | bytes 9437184

commit v2 on v1

v2 whole, which is shorter than its diff:
```python
import jax
import jax.numpy as jnp
from jax import lax
from jax.experimental import pallas as pl
from jax.experimental.pallas import tpu as pltpu
from jax.sharding import PartitionSpec as P

N_GEN = 2
STEP = 100
MESH = pl.DeviceIdType.MESH
BF16, F32 = jnp.bfloat16, jnp.float32

X, Z, Y = 4, 8, 4
LANES = 128
HALF = 72
PIECE = 2 * HALF
BLOCKS = 9
OFFSETS = (2, 1, 3, 0)

LATENCY, PIECE_US, STEP_US = 2.2, 0.39, 0.12


def in_order(steps):
    left = {}

    def ahead(name):
        if name not in left:
            later = [
                ahead(other) + (LATENCY + PIECE_US if how == "sent" else 0.0)
                for other, (_, needs, _) in steps.items()
                for how, needed in needs
                if needed == name
            ]
            left[name] = steps[name][0] + max(later, default=0.0)
        return left[name]

    for name in steps:
        ahead(name)
    now, link_free, done, arrived, order = 0.0, {}, {}, {}, []
    while len(order) < len(steps):
        ready = []
        for name, (_, needs, _) in steps.items():
            if name in done:
                continue
            times = [(done if how == "done" else arrived).get(needed) for how, needed in needs]
            if None not in times:
                ready.append((max(times, default=0.0), -left[name], name))
        able = [(key, when, name) for when, key, name in ready if when <= now]
        if not able:
            now = min(ready)[0]
            continue
        name = min(able)[2]
        now += steps[name][0]
        done[name] = now
        for link, pieces in steps[name][2].items():
            link_free[link] = max(link_free.get(link, 0.0), now) + PIECE_US * pieces
            arrived[name] = max(arrived.get(name, 0.0), link_free[link] + LATENCY)
        order.append(name)
    return order, now


CHAIN = (4, 3, -3, 2, -2, 1, -1)
ROLES = ("far", "plus", "minus", "mine")


def before(k):
    return None if k in (4, -3) else k + 1 if k > 0 else k - 1


def sum_steps():
    steps = {}
    for t in range(X):
        steps["mul", t] = (1.4, [("done", ("mul", t - 1))] if t else [], {"core%d" % t: 0.5})

    def have(*blocks):
        return [("sent", ("mul", t)) for t in blocks]

    for k in CHAIN + (0,):
        steps["a1", "far", k] = (STEP_US, have(0), {"x": 1})
        steps["a1", "minus", k] = (STEP_US, have(1, 2), {"x": 1})
        steps["a1", "plus", k] = (STEP_US, have(1, 2) + [("sent", ("a1", "far", k))], {"x": 1})
        needs = have(3) + [("sent", ("a1", "plus", k)), ("sent", ("a1", "minus", k))]
        if k == 0:
            needs += [("sent", ("a2", 1)), ("sent", ("a2", -1))]
        elif before(k) is not None:
            needs.append(("sent", ("a2", before(k))))
        steps["a2", k] = (STEP_US, needs, {"z": 1} if k else {})
    for role in ROLES:
        block = {"far": (0,), "plus": (1, 2), "minus": (1, 2), "mine": (3,)}[role]
        for k in CHAIN:
            needs = have(*block)
            if before(k) is not None:
                needs.append(("sent", ("b1", role, before(k))))
            steps["b1", role, k] = (STEP_US, needs, {"z": 1})
        needs = have(*block) + [("sent", ("b1", role, 1)), ("sent", ("b1", role, -1))]
        needs += {
            "far": [], "minus": [], "plus": [("sent", ("b2", "far"))],
            "mine": [("sent", ("b2", "plus")), ("sent", ("b2", "minus"))],
        }[role]
        steps["b2", role] = (STEP_US, needs, {} if role == "mine" else {"x": 1})
    return steps


def gather_steps():
    steps = {}
    places = (0, -1, 1, -2, 2, -3, 3, -4)
    for k in places:
        links = {}
        for i in (0, -1, 1, -2):
            if i == 0:
                needs = [] if k == 0 else [("sent", ("wa", 0, k + 1 if k < 0 else k - 1))]
                links = {"z": (2 if k == 0 else 1 if k in (-1, -2, -3, 1, 2) else 0), "x": 2}
            else:
                needs = [("sent", ("wa", i + 1 if i < 0 else i - 1, k))]
                links = {"x": 1 if i == -1 else 0}
            steps["wa", i, k] = (STEP_US, needs, links)
            if k == 0:
                needs = [] if i == 0 else [("sent", ("wb", i + 1 if i < 0 else i - 1, 0))]
                links = {"x": (2 if i == 0 else 1 if i == -1 else 0), "z": 2}
            else:
                needs = [("sent", ("wb", i, k + 1 if k < 0 else k - 1))]
                links = {"z": 1 if k in (-1, -2, -3, 1, 2) else 0}
            steps["wb", i, k] = (STEP_US, needs, links)
    return steps


def numbered(names, start):
    return {name: start + n for n, name in enumerate(names)}


S_CORE = 0
S_SUM = numbered([name for name in sum_steps() if name[0] != "mul" and name not in (("a2", 0), ("b2", "mine"))], 4)
S_G = 4 + len(S_SUM)
S_H = S_G + 7
S_WAY = numbered(
    [name + (way,) for name in gather_steps() for way in ("z_next", "z_last", "x_next", "x_last")], 0
)
N_SUM = len(S_SUM)

L_ACTS = 0
L_COT = L_ACTS + 4
L_STATE = L_COT + 2
L_NEW = L_STATE + 4
L_OUT = L_NEW + 1
N_LOCAL = L_OUT + 24


def kernel(
    acts, cot, params, moment1, moment2, ema, live_rows, home, new_state, refreshed,
    acts_buf, cot_buf, own, core_out, core_in, sum_out, sum_in,
    g_out, g_in, g_all, state, fresh, h_all, h_out, h_in, w_all, w_mine, gathered,
    position, order, send_sems, recv_sems, way_send, way_recv, local_sems,
):
    dp = lax.axis_index("dp")
    y = lax.axis_index("section")
    c = lax.rem(dp, 2)
    z = lax.rem(lax.div(dp, 2), Z)
    x = lax.div(dp, 2 * Z)
    sign = 1 - 2 * c

    def xi(k):
        return lax.rem(x + sign * k + 2 * X, X)

    def zi(k):
        return lax.rem(z + sign * k + 2 * Z, Z)

    def at(xx, zz, cc, yy):
        return ((xx * Z + zz) * 2 + cc, yy)

    x_next, x_last = at(xi(1), z, c, y), at(xi(-1), z, c, y)
    z_next, z_last = at(x, zi(1), c, y), at(x, zi(-1), c, y)
    partner = at(x, z, 1 - c, y)
    others = []
    for dy in range(Y):
        for dc in range(2):
            if dy or dc:
                others.append((lax.rem(c + dc, 2), lax.rem(y + dy, Y)))

    barrier = pltpu.get_barrier_semaphore()
    greeted = [x_next, x_last, z_next, z_last] + [at(x, z, cc, yy) for cc, yy in others]
    for device in greeted:
        pl.semaphore_signal(barrier, inc=1, device_id=device, device_id_type=MESH)

    pending = []

    def local(src, dst, index):
        copy = pltpu.make_async_copy(src, dst, local_sems.at[index])
        copy.start()
        return copy

    def send(src, dst, device, sent, arrived):
        copy = pltpu.make_async_remote_copy(
            src_ref=src, dst_ref=dst, send_sem=sent, recv_sem=arrived,
            device_id=device, device_id_type=MESH,
        )
        copy.start()
        pending.append(copy)
        return copy

    width = Z * PIECE
    cot_copies = []
    for half in range(2):
        column = pl.multiple_of(256 * lax.rem(c + half, 2), 256)
        cot_copies.append(
            local(cot.at[:, pl.ds(column, 256)], cot_buf.at[:, pl.ds(256 * half, 256)], L_COT + half)
        )
    for t, offset in enumerate(OFFSETS):
        column = pl.multiple_of(width * lax.rem(x + offset, X), LANES)
        local(acts.at[:, pl.ds(column, width)], acts_buf.at[t], L_ACTS + t)
    state_copies = [
        local(ref, state.at[n], L_STATE + n) for n, ref in enumerate((params, moment1, moment2, ema))
    ]

    def section_row(s, carry):
        def block_entry(b, carry):
            counts, kept = carry[:Y], carry[Y:]
            keeper = home[s, b]
            rank = jnp.int32(0)
            for n in range(Y):
                rank = jnp.where(keeper == n, counts[n], rank)
            place = keeper * BLOCKS + rank
            position[s * BLOCKS + b] = place
            counts = tuple(counts[n] + jnp.where(keeper == n, 1, 0) for n in range(Y))
            here = place - y * BLOCKS
            kept = tuple(jnp.where(here == n, s * BLOCKS + b, kept[n]) for n in range(BLOCKS))
            return counts + kept

        return lax.fori_loop(0, BLOCKS, block_entry, carry)

    table = lax.fori_loop(0, Y, section_row, (jnp.int32(0),) * (Y + BLOCKS))
    for n in range(BLOCKS):
        order[n] = table[Y + n]

    pl.semaphore_wait(barrier, len(greeted))

    for copy in cot_copies:
        copy.wait()

    def core_copy(t):
        return pltpu.make_async_remote_copy(
            src_ref=core_out.at[t], dst_ref=core_in.at[t],
            send_sem=send_sems.at[S_CORE + t], recv_sem=recv_sems.at[S_CORE + t],
            device_id=partner, device_id_type=MESH,
        )

    def multiply(t):
        pltpu.make_async_copy(
            acts.at[:, pl.ds(0, width)], acts_buf.at[t], local_sems.at[L_ACTS + t]
        ).wait()
        product = lax.dot_general(
            acts_buf[t], cot_buf[...], (((0,), (0,)), ((), ())), preferred_element_type=F32
        )
        for h in range(2):
            own[t, h] = product[:, LANES * h : LANES * (h + 1)].reshape(Z, PIECE, LANES)
            other = product[:, 256 + LANES * h : 256 + LANES * (h + 1)]
            core_out[t, h] = other.reshape(Z, PIECE, LANES).astype(BF16)
        copy = core_copy(t)
        copy.start()
        pending.append(copy)

    here = {"far": 0, "plus": 1 + c, "minus": 2 - c, "mine": 3}
    needed = {"far": (0,), "plus": (1, 2), "minus": (1, 2), "mine": (3,)}
    crossed, moving = set(), {}

    def block(h, role, k):
        for t in needed[role]:
            if t not in crossed:
                core_copy(t).wait_recv()
                crossed.add(t)
        return own[here[role], h, zi(k)] + core_in[here[role], h, zi(k)].astype(F32)

    def taken(name):
        moving[name].wait_recv()
        return sum_in[S_SUM[name] - 4].astype(F32)

    def give(name, value, device):
        slot = S_SUM[name] - 4
        sum_out[slot] = value.astype(BF16)
        moving[name] = send(
            sum_out.at[slot], sum_in.at[slot], device, send_sems.at[S_SUM[name]], recv_sems.at[S_SUM[name]]
        )

    def along_x(role):
        return x_last if role == "minus" else x_next

    def along_z(k):
        return z_next if k > 0 else z_last

    for name in in_order(sum_steps())[0]:
        if name[0] == "mul":
            multiply(name[1])
        elif name[0] == "a1":
            _, role, k = name
            value = block(0, role, k)
            if role == "plus":
                value = value + taken(("a1", "far", k))
            give(name, value, along_x(role))
        elif name[0] == "a2":
            k = name[1]
            value = block(0, "mine", k) + taken(("a1", "minus", k)) + taken(("a1", "plus", k))
            for earlier in (1, -1) if k == 0 else () if before(k) is None else (before(k),):
                value = value + taken(("a2", earlier))
            if k == 0:
                sum_a = value
            else:
                give(name, value, along_z(k))
        elif name[0] == "b1":
            _, role, k = name
            value = block(1, role, k)
            if before(k) is not None:
                value = value + taken(("b1", role, before(k)))
            give(name, value, along_z(k))
        else:
            role = name[1]
            value = block(1, role, 0) + taken(("b1", role, 1)) + taken(("b1", role, -1))
            for earlier in {"plus": ("far",), "mine": ("plus", "minus")}.get(role, ()):
                value = value + taken(("b2", earlier))
            if role == "mine":
                sum_b = value
            else:
                give(name, value, along_x(role))

    mine = 2 * y + c

    def spread(out, into, base):
        into[mine] = out[c]
        copies = []
        for n, (cc, yy) in enumerate(others):
            copies.append(
                send(
                    out.at[cc], into.at[mine], at(x, z, cc, yy), send_sems.at[base + n], recv_sems.at[base + n]
                )
            )
        for copy in copies:
            copy.wait_recv()

    for cc in range(2):
        rows = slice(HALF * cc, HALF * (cc + 1))
        g_out[cc] = jnp.concatenate([sum_a[rows], sum_b[rows]], axis=0).astype(BF16)
    spread(g_out, g_in, S_G)
    for s in range(Y):
        for cc in range(2):
            value = g_in[2 * s + cc].astype(F32)
            for jj in range(2):
                g_all[2 * cc + jj, BLOCKS * s : BLOCKS * (s + 1)] = value[HALF * jj : HALF * (jj + 1)].reshape(
                    BLOCKS, 8, LANES
                )

    for copy in state_copies:
        copy.wait()
    corr_one = 1.0 - 0.9**STEP
    corr_two = 1.0 - 0.99**STEP

    @pl.loop(0, BLOCKS)
    def _(i):
        f = order[i]
        s = lax.div(f, BLOCKS)
        b = f - s * BLOCKS
        limit = live_rows[s] - (dp * (4 * HALF) + b * 32)
        tile = lax.broadcasted_iota(jnp.int32, (8, LANES), 0)
        generator = tile * 0 + s < N_GEN
        for j in range(4):
            rows = pl.ds(i * 32 + j, 8, stride=4)
            grads = g_all[j, f]
            alive = tile * 4 + j < limit
            p, m1, m2, average = (state[n, rows, :] for n in range(4))
            first = jnp.where(alive, 0.9 * m1 + 0.1 * grads, m1)
            second = jnp.where(alive, 0.99 * m2 + 0.01 * grads * grads, m2)
            stepped = p - 0.0025 * (first / corr_one) / (jnp.sqrt(second / corr_two) + 1e-08)
            updated = jnp.where(alive, stepped, p)
            averaged = jnp.where(generator, 0.995 * average + 0.005 * updated, average)
            for n, value in enumerate((updated, first, second, averaged)):
                fresh[n, rows, :] = value
            h_all[j, pl.ds(pl.multiple_of(i * 8, 8), 8), :] = updated

    for cc in range(2):
        h_out[cc] = h_all[2 * cc : 2 * cc + 2].reshape(PIECE, LANES).astype(BF16)
    spread(h_out, h_in, S_H)
    fresh_copy = local(fresh, new_state, L_NEW)
    for s in range(Y):
        for cc in range(2):
            value = h_in[2 * s + cc].astype(F32)
            for jj in range(2):
                w_all[jj, cc, BLOCKS * s : BLOCKS * (s + 1)] = value[HALF * jj : HALF * (jj + 1)].reshape(
                    BLOCKS, 8, LANES
                )

    @pl.loop(0, BLOCKS)
    def _(b):
        place = position[y * BLOCKS + b]
        for cc in range(2):
            for jj in range(2):
                w_mine[jj, pl.ds(pl.multiple_of(HALF * cc + b * 8, 8), 8), :] = w_all[jj, cc, place]

    ja, jb = 2 * c, 2 * c + 1
    gathered[ja, x, z] = w_mine[0].astype(BF16)
    gathered[jb, x, z] = w_mine[1].astype(BF16)
    halves = {"wa": ja, "wb": jb}
    ways = {"z_next": z_next, "z_last": z_last, "x_next": x_next, "x_last": x_last}

    def go(name, way):
        _, i, k = name
        ref = gathered.at[halves[name[0]], xi(i), zi(k)]
        number = S_WAY[name + (way,)]
        moving[name + (way,)] = send(ref, ref, ways[way], way_send.at[number], way_recv.at[number])

    def comes(name, axis, i):
        back = i + 1 if i < 0 else i - 1
        at_sender = (name[0], back, name[2]) if axis == "x" else (name[0], name[1], back)
        moving[at_sender + (axis + ("_next" if i < 0 else "_last"),)].wait_recv()

    def onward(axis, i, size):
        if i == 0:
            return [axis + "_next", axis + "_last"]
        if i < 0:
            return [axis + "_next"] if i > -(size // 2) else []
        return [axis + "_last"] if i < size // 2 - 1 else []

    seen, crossing, written = [], {}, []

    def write(j, xx, zz):
        lanes = pl.ds(pl.multiple_of(j * LANES, LANES), LANES)
        if xx is not None:
            source, target = gathered.at[j, xx], refreshed.at[xx, :, :, lanes]
        else:
            source, target = gathered.at[j, :, zz], refreshed.at[:, zz, :, lanes]
        written.append(local(source, target, L_OUT + len(written)))

    def cross(half, i, k):
        number = len(crossing)
        write(halves[half], None if half == "wb" else xi(i), zi(k))
        ref = gathered.at[halves[half], xi(i)] if half == "wa" else gathered.at[halves[half], :, zi(k)]
        crossing[half, i, k] = send(ref, ref, partner, send_sems.at[S_H + 7 + number], recv_sems.at[S_H + 7 + number])

    for name in in_order(gather_steps())[0]:
        half, i, k = name
        first, second = (("z", k, Z), ("x", i, X)) if half == "wa" else (("x", i, X), ("z", k, Z))
        if second[1] != 0:
            comes(name, *second[:2])
            moves = onward(*second)
        else:
            if first[1] != 0:
                comes(name, *first[:2])
            moves = onward(*first) + onward(*second)
        for way in moves:
            go(name, way)
        seen.append(name)
        if half == "wa" and sum(n[:2] == name[:2] for n in seen) == Z:
            cross("wa", i, 0)
        if half == "wb" and sum(n[0] == "wb" and n[2] == k for n in seen) == X:
            cross("wb", 0, k)

    for (half, i, k), copy in crossing.items():
        copy.wait_recv()
        write(2 * (1 - c) + (half == "wb"), None if half == "wb" else xi(-i), zi(-k))
    for copy in written:
        copy.wait()
    fresh_copy.wait()
    for copy in pending:
        copy.wait_send()


def write_out(
    new_state, refreshed, new_params, new_moment1, new_moment2, new_ema, weights, state_buf, buf, in_sems, out_sems
):
    moves = [
        (new_state.at[n], state_buf.at[n], ref)
        for n, ref in enumerate((new_params, new_moment1, new_moment2, new_ema))
    ]
    for xx in range(X):
        for half in range(2):
            part = pl.ds(4 * half, 4)
            moves.append((refreshed.at[xx, part], buf.at[xx, part], weights.at[xx, part]))
    first = [pltpu.make_async_copy(a, b, in_sems.at[n]) for n, (a, b, _) in enumerate(moves)]
    second = [pltpu.make_async_copy(b, d, out_sems.at[n]) for n, (_, b, d) in enumerate(moves)]
    for copy in first:
        copy.start()
    for arrived, copy in zip(first, second):
        arrived.wait()
        copy.start()
    for copy in second:
        copy.wait()


def body(acts, grad_out, params, moment1, moment2, ema, live_rows, home):
    tokens = acts.shape[1]
    rows = (4 * HALF, LANES)
    any_space = pl.BlockSpec(memory_space=pl.ANY)
    smem = pl.BlockSpec(memory_space=pltpu.SMEM)
    plane = (Z, PIECE, LANES)
    chunk = (PIECE, LANES)
    outs = pl.pallas_call(
        kernel,
        out_shape=[
            jax.ShapeDtypeStruct((4,) + rows, F32),
            jax.ShapeDtypeStruct((X, Z, PIECE, 4 * LANES), BF16),
        ],
        in_specs=[any_space] * 6 + [smem] * 2,
        out_specs=[any_space] * 2,
        scratch_shapes=[
            pltpu.VMEM((X, tokens, Z * PIECE), BF16),
            pltpu.VMEM((tokens, 4 * LANES), BF16),
            pltpu.VMEM((X, 2) + plane, F32),
            pltpu.VMEM((X, 2) + plane, BF16),
            pltpu.VMEM((X, 2) + plane, BF16),
            pltpu.VMEM((N_SUM,) + chunk, BF16),
            pltpu.VMEM((N_SUM,) + chunk, BF16),
            pltpu.VMEM((2,) + chunk, BF16),
            pltpu.VMEM((2 * Y,) + chunk, BF16),
            pltpu.VMEM((4, Y * BLOCKS, 8, LANES), F32),
            pltpu.VMEM((4,) + rows, F32),
            pltpu.VMEM((4,) + rows, F32),
            pltpu.VMEM((4, HALF, LANES), F32),
            pltpu.VMEM((2,) + chunk, BF16),
            pltpu.VMEM((2 * Y,) + chunk, BF16),
            pltpu.VMEM((2, 2, Y * BLOCKS, 8, LANES), F32),
            pltpu.VMEM((2,) + chunk, F32),
            pltpu.VMEM((4, X) + plane, BF16),
            pltpu.SMEM((Y * BLOCKS,), jnp.int32),
            pltpu.SMEM((BLOCKS,), jnp.int32),
            pltpu.SemaphoreType.DMA((S_H + 19,)),
            pltpu.SemaphoreType.DMA((S_H + 19,)),
            pltpu.SemaphoreType.DMA((len(S_WAY),)),
            pltpu.SemaphoreType.DMA((len(S_WAY),)),
            pltpu.SemaphoreType.DMA((N_LOCAL,)),
        ],
        compiler_params=pltpu.CompilerParams(
            collective_id=0, has_side_effects=True, vmem_limit_bytes=56 * 2**20
        ),
    )(acts[0], grad_out[0], params[0], moment1[0], moment2[0], ema[0], live_rows, home)
    updated, first, second, averaged, weights = pl.pallas_call(
        write_out,
        out_shape=[jax.ShapeDtypeStruct(rows, F32)] * 4
        + [jax.ShapeDtypeStruct((X, Z, PIECE, 4 * LANES), BF16)],
        in_specs=[any_space] * 2,
        out_specs=[any_space] * 5,
        scratch_shapes=[
            pltpu.VMEM((4,) + rows, F32),
            pltpu.VMEM((X, Z, PIECE, 4 * LANES), BF16),
            pltpu.SemaphoreType.DMA((4 + 2 * X,)),
            pltpu.SemaphoreType.DMA((4 + 2 * X,)),
        ],
        compiler_params=pltpu.CompilerParams(vmem_limit_bytes=56 * 2**20),
    )(*outs)
    return (
        updated[None], first[None], second[None], averaged[None],
        weights.reshape(1, X * Z * PIECE, 4 * LANES),
    )


def solution(mesh):
    split = P("section", "dp", None)
    in_specs = (split,) * 6 + (P(), P())
    out_specs = (split,) * 4 + (P("section", None, None),)
    return jax.shard_map(body, mesh=mesh, in_specs=in_specs, out_specs=out_specs, check_vma=False)
```

time: 104 us -> 84.2 us (0.81)
  local copies, waits for them, and re-layouts: 11.1 us -> 0 us
  Pallas kernels: 92.2 us -> 83.5 us
    unnamed x5 -> x0, local copies, waits for them, and re-layouts: 11.1 us -> none
    pallas_call x1 -> x2, Pallas kernels: 92.2 us -> 83.5 us  [the longest x1 78.5 us: body(): pl.pallas_call(kernel, out_shape=[jax.ShapeDtypeStruct((4,) + rows, F32),...]
where the time goes in v2:
time: 84.2 us; the launch traced here: 84.1 us
  Pallas kernels  83.5 us (99%)
    pallas_call x1, Pallas kernels, body(): pl.pallas_call(kernel, out_shape=[jax.ShapeDtypeStruct((4,) + rows, F32),...  78.5 us
    pallas_call x1, Pallas kernels, body(): pl.pallas_call(write_out, out_shape=[jax.ShapeDtypeStruct(rows, F32)] * 4...  4.98 us

profile of v2, /device:TPU:1, one launch (start us, length us, event | category | flops | bytes accessed | tf_op | source)
XLA Modules:
  0.0 84.1 jit_solution(5851124211564373562)
XLA Ops:
  0.6 78.5 %shard_map.119 = (f32[4,288,128]{2,1,0:T(8,128)}, bf16[4,8,144,512]{3,2,1,0:T(8,128)(2,1)}) custom-call(bf16[768,4608]{1,0:T(8,128)(2,1)} %bitcast.11, bf16[768,512]{1,0:T(8,128)(2,1)} %bitcast.12, f32[288,128]{1,0:T(8,128)} %bitcast.13, f32[288,128]{1,0:T(8,128)} %bitcast.14, f32[288,128]{1,0:T(8,128)} %bitcast.15, f32[288,128]{1,0:T(8,128)} %bitcast.16, ...), custom_call_target="tpu_custom_call" | custom-call | tf_op jit(solution)/shard_map/pallas_call | solution.py:492
  79.1 5.0 %shard_map.120 = (f32[288,128]{1,0:T(8,128)}, f32[288,128]{1,0:T(8,128)}, f32[288,128]{1,0:T(8,128)}, f32[288,128]{1,0:T(8,128)}, bf16[4,8,144,512]{3,2,1,0:T(8,128)(2,1)}) custom-call(f32[4,288,128]{2,1,0:T(8,128)} %get-tuple-element.12.new_state, bf16[4,8,144,512]{3,2,1,0:T(8,128)(2,1)} %get-tuple-element.13.refreshed), custom_call_target="tpu_custom_call" | custom-call | tf_op jit(solution)/shard_map/pallas_call | solution.py:531

commit v3 on v2

--- a/solution.py
+++ b/solution.py
@@ -128,14 +128,30 @@
     return {name: start + n for n, name in enumerate(names)}
 
 
-S_CORE = 0
-S_SUM = numbered([name for name in sum_steps() if name[0] != "mul" and name not in (("a2", 0), ("b2", "mine"))], 4)
-S_G = 4 + len(S_SUM)
-S_H = S_G + 7
-S_WAY = numbered(
-    [name + (way,) for name in gather_steps() for way in ("z_next", "z_last", "x_next", "x_last")], 0
-)
-N_SUM = len(S_SUM)
+def onward(axis, i, size):
+    if i == 0:
+        return [axis + "_next", axis + "_last"]
+    if i < 0:
+        return [axis + "_next"] if i > -(size // 2) else []
+    return [axis + "_last"] if i < size // 2 - 1 else []
+
+
+def ways_on(name):
+    half, i, k = name
+    if half == "wa":
+        return (onward("z", k, Z) if i == 0 else []) + onward("x", i, X)
+    return (onward("x", i, X) if k == 0 else []) + onward("z", k, Z)
+
+
+R_CORE = 0
+R_SUM = numbered([name for name in sum_steps() if name[0] != "mul" and name not in (("a2", 0), ("b2", "mine"))], 4)
+N_SUM = len(R_SUM)
+R_G = 4 + N_SUM
+R_H = R_G + 7
+R_CROSS = R_H + 7
+R_WAY = numbered([name + (way,) for name in gather_steps() for way in ways_on(name)], R_CROSS + 12)
+N_ARRIVE = R_CROSS + 12 + len(R_WAY)
+S_CORE, S_SUM, S_G, S_H, S_WAY, S_ROW, S_COLUMN = range(7)
 
 L_ACTS = 0
 L_COT = L_ACTS + 4
@@ -149,7 +165,7 @@
     acts, cot, params, moment1, moment2, ema, live_rows, home, new_state, refreshed,
     acts_buf, cot_buf, own, core_out, core_in, sum_out, sum_in,
     g_out, g_in, g_all, state, fresh, h_all, h_out, h_in, w_all, w_mine, gathered,
-    position, order, send_sems, recv_sems, way_send, way_recv, local_sems,
+    position, order, send_sems, recv_sems, local_sems,
 ):
     dp = lax.axis_index("dp")
     y = lax.axis_index("section")
@@ -181,20 +197,17 @@
     for device in greeted:
         pl.semaphore_signal(barrier, inc=1, device_id=device, device_id_type=MESH)
 
-    pending = []
-
     def local(src, dst, index):
         copy = pltpu.make_async_copy(src, dst, local_sems.at[index])
         copy.start()
         return copy
 
-    def send(src, dst, device, sent, arrived):
+    def send(src, dst, device, group, number):
         copy = pltpu.make_async_remote_copy(
-            src_ref=src, dst_ref=dst, send_sem=sent, recv_sem=arrived,
+            src_ref=src, dst_ref=dst, send_sem=send_sems.at[group], recv_sem=recv_sems.at[number],
             device_id=device, device_id_type=MESH,
         )
         copy.start()
-        pending.append(copy)
         return copy
 
     width = Z * PIECE
@@ -211,26 +224,6 @@
         local(ref, state.at[n], L_STATE + n) for n, ref in enumerate((params, moment1, moment2, ema))
     ]
 
-    def section_row(s, carry):
-        def block_entry(b, carry):
-            counts, kept = carry[:Y], carry[Y:]
-            keeper = home[s, b]
-            rank = jnp.int32(0)
-            for n in range(Y):
-                rank = jnp.where(keeper == n, counts[n], rank)
-            place = keeper * BLOCKS + rank
-            position[s * BLOCKS + b] = place
-            counts = tuple(counts[n] + jnp.where(keeper == n, 1, 0) for n in range(Y))
-            here = place - y * BLOCKS
-            kept = tuple(jnp.where(here == n, s * BLOCKS + b, kept[n]) for n in range(BLOCKS))
-            return counts + kept
-
-        return lax.fori_loop(0, BLOCKS, block_entry, carry)
-
-    table = lax.fori_loop(0, Y, section_row, (jnp.int32(0),) * (Y + BLOCKS))
-    for n in range(BLOCKS):
-        order[n] = table[Y + n]
-
     pl.semaphore_wait(barrier, len(greeted))
 
     for copy in cot_copies:
@@ -239,11 +232,51 @@
     def core_copy(t):
         return pltpu.make_async_remote_copy(
             src_ref=core_out.at[t], dst_ref=core_in.at[t],
-            send_sem=send_sems.at[S_CORE + t], recv_sem=recv_sems.at[S_CORE + t],
+            send_sem=send_sems.at[S_CORE], recv_sem=recv_sems.at[R_CORE + t],
             device_id=partner, device_id_type=MESH,
         )
 
-    def multiply(t):
+    here = {"far": 0, "plus": 1 + c, "minus": 2 - c, "mine": 3}
+    needed = {"far": (0,), "plus": (1, 2), "minus": (1, 2), "mine": (3,)}
+    crossed, moving = {0}, {}
+
+    def block(h, role, k):
+        for t in needed[role]:
+            if t not in crossed:
+                core_copy(t).wait_recv()
+                crossed.add(t)
+        return own[here[role], h, zi(k)] + core_in[here[role], h, zi(k)].astype(F32)
+
+    def taken(name):
+        moving[name].wait_recv()
+        return sum_in[R_SUM[name] - 4].astype(F32)
+
+    def piece_copy(name, device):
+        slot = R_SUM[name] - 4
+        return pltpu.make_async_remote_copy(
+            src_ref=sum_out.at[slot], dst_ref=sum_in.at[slot],
+            send_sem=send_sems.at[S_SUM], recv_sem=recv_sems.at[R_SUM[name]],
+            device_id=device, device_id_type=MESH,
+        )
+
+    def remember(name, device):
+        moving[name] = piece_copy(name, device)
+
+    def give(name, value, device):
+        sum_out[R_SUM[name] - 4] = value.astype(BF16)
+        piece_copy(name, device).start()
+        remember(name, device)
+
+    def along_x(role):
+        return x_last if role == "minus" else x_next
+
+    def along_z(k):
+        return z_next if k > 0 else z_last
+
+    early = [("a1", "far", k) for k in CHAIN + (0,)] + [("b1", "far", 4), ("b1", "far", -3)]
+
+    @pl.loop(0, X)
+    def _(t):
         pltpu.make_async_copy(
             acts.at[:, pl.ds(0, width)], acts_buf.at[t], local_sems.at[L_ACTS + t]
         ).wait()
@@ -254,42 +287,24 @@
             own[t, h] = product[:, LANES * h : LANES * (h + 1)].reshape(Z, PIECE, LANES)
             other = product[:, 256 + LANES * h : 256 + LANES * (h + 1)]
             core_out[t, h] = other.reshape(Z, PIECE, LANES).astype(BF16)
-        copy = core_copy(t)
-        copy.start()
-        pending.append(copy)
-
-    here = {"far": 0, "plus": 1 + c, "minus": 2 - c, "mine": 3}
-    needed = {"far": (0,), "plus": (1, 2), "minus": (1, 2), "mine": (3,)}
-    crossed, moving = set(), {}
-
-    def block(h, role, k):
-        for t in needed[role]:
-            if t not in crossed:
-                core_copy(t).wait_recv()
-                crossed.add(t)
-        return own[here[role], h, zi(k)] + core_in[here[role], h, zi(k)].astype(F32)
-
-    def taken(name):
-        moving[name].wait_recv()
-        return sum_in[S_SUM[name] - 4].astype(F32)
-
-    def give(name, value, device):
-        slot = S_SUM[name] - 4
-        sum_out[slot] = value.astype(BF16)
-        moving[name] = send(
-            sum_out.at[slot], sum_in.at[slot], device, send_sems.at[S_SUM[name]], recv_sems.at[S_SUM[name]]
-        )
-
-    def along_x(role):
-        return x_last if role == "minus" else x_next
-
-    def along_z(k):
-        return z_next if k > 0 else z_last
+        core_copy(t).start()
+
+        @pl.when(t == 1)
+        def _():
+            core_copy(0).wait_recv()
+            for name in early:
+                half, role, k = name
+                value = block(0 if half == "a1" else 1, role, k)
+                sum_out[R_SUM[name] - 4] = value.astype(BF16)
+                piece_copy(name, x_next if half == "a1" else along_z(k)).start()
+
+    for name in early:
+        remember(name, x_next if name[0] == "a1" else along_z(name[2]))
 
     for name in in_order(sum_steps())[0]:
-        if name[0] == "mul":
-            multiply(name[1])
-        elif name[0] == "a1":
+        if name[0] == "mul" or name in early:
+            continue
+        if name[0] == "a1":
             _, role, k = name
             value = block(0, role, k)
             if role == "plus":
@@ -322,22 +337,43 @@
 
     mine = 2 * y + c
 
-    def spread(out, into, base):
+    def spread(out, into, group, base, meanwhile=None):
         into[mine] = out[c]
         copies = []
         for n, (cc, yy) in enumerate(others):
             copies.append(
-                send(
-                    out.at[cc], into.at[mine], at(x, z, cc, yy), send_sems.at[base + n], recv_sems.at[base + n]
-                )
+                send(out.at[cc], into.at[mine], at(x, z, cc, yy), group, base + n)
             )
+        if meanwhile is not None:
+            meanwhile()
         for copy in copies:
             copy.wait_recv()
+
+    def read_table():
+        def section_row(s, carry):
+            def block_entry(b, carry):
+                counts, kept = carry[:Y], carry[Y:]
+                keeper = home[s, b]
+                rank = jnp.int32(0)
+                for n in range(Y):
+                    rank = jnp.where(keeper == n, counts[n], rank)
+                place = keeper * BLOCKS + rank
+                position[s * BLOCKS + b] = place
+                counts = tuple(counts[n] + jnp.where(keeper == n, 1, 0) for n in range(Y))
+                here = place - y * BLOCKS
+                kept = tuple(jnp.where(here == n, s * BLOCKS + b, kept[n]) for n in range(BLOCKS))
+                return counts + kept
+
+            return lax.fori_loop(0, BLOCKS, block_entry, carry)
+
+        table = lax.fori_loop(0, Y, section_row, (jnp.int32(0),) * (Y + BLOCKS))
+        for n in range(BLOCKS):
+            order[n] = table[Y + n]
 
     for cc in range(2):
         rows = slice(HALF * cc, HALF * (cc + 1))
         g_out[cc] = jnp.concatenate([sum_a[rows], sum_b[rows]], axis=0).astype(BF16)
-    spread(g_out, g_in, S_G)
+    spread(g_out, g_in, S_G, R_G, read_table)
     for s in range(Y):
         for cc in range(2):
             value = g_in[2 * s + cc].astype(F32)
@@ -375,7 +411,7 @@
 
     for cc in range(2):
         h_out[cc] = h_all[2 * cc : 2 * cc + 2].reshape(PIECE, LANES).astype(BF16)
-    spread(h_out, h_in, S_H)
+    spread(h_out, h_in, S_H, R_H)
     fresh_copy = local(fresh, new_state, L_NEW)
     for s in range(Y):
         for cc in range(2):
@@ -401,20 +437,12 @@
     def go(name, way):
         _, i, k = name
         ref = gathered.at[halves[name[0]], xi(i), zi(k)]
-        number = S_WAY[name + (way,)]
-        moving[name + (way,)] = send(ref, ref, ways[way], way_send.at[number], way_recv.at[number])
+        moving[name + (way,)] = send(ref, ref, ways[way], S_WAY, R_WAY[name + (way,)])
 
     def comes(name, axis, i):
         back = i + 1 if i < 0 else i - 1
         at_sender = (name[0], back, name[2]) if axis == "x" else (name[0], name[1], back)
         moving[at_sender + (axis + ("_next" if i < 0 else "_last"),)].wait_recv()
-
-    def onward(axis, i, size):
-        if i == 0:
-            return [axis + "_next", axis + "_last"]
-        if i < 0:
-            return [axis + "_next"] if i > -(size // 2) else []
-        return [axis + "_last"] if i < size // 2 - 1 else []
 
     seen, crossing, written = [], {}, []
 
@@ -430,19 +458,16 @@
         number = len(crossing)
         write(halves[half], None if half == "wb" else xi(i), zi(k))
         ref = gathered.at[halves[half], xi(i)] if half == "wa" else gathered.at[halves[half], :, zi(k)]
-        crossing[half, i, k] = send(ref, ref, partner, send_sems.at[S_H + 7 + number], recv_sems.at[S_H + 7 + number])
+        crossing[half, i, k] = send(ref, ref, partner, S_ROW if half == "wa" else S_COLUMN, R_CROSS + number)
 
     for name in in_order(gather_steps())[0]:
         half, i, k = name
-        first, second = (("z", k, Z), ("x", i, X)) if half == "wa" else (("x", i, X), ("z", k, Z))
+        first, second = (("z", k), ("x", i)) if half == "wa" else (("x", i), ("z", k))
         if second[1] != 0:
-            comes(name, *second[:2])
-            moves = onward(*second)
-        else:
-            if first[1] != 0:
-                comes(name, *first[:2])
-            moves = onward(*first) + onward(*second)
-        for way in moves:
+            comes(name, *second)
+        elif first[1] != 0:
+            comes(name, *first)
+        for way in ways_on(name):
             go(name, way)
         seen.append(name)
         if half == "wa" and sum(n[:2] == name[:2] for n in seen) == Z:
@@ -456,8 +481,12 @@
     for copy in written:
         copy.wait()
     fresh_copy.wait()
-    for copy in pending:
-        copy.wait_send()
+
+    for group, ref in (
+        (S_CORE, core_out), (S_SUM, sum_out), (S_G, g_in.at[pl.ds(0, 7)]), (S_H, h_in.at[pl.ds(0, 7)]),
+        (S_WAY, sum_out), (S_ROW, gathered.at[0]), (S_COLUMN, gathered.at[0]),
+    ):
+        pltpu.make_async_copy(ref, ref, send_sems.at[group]).wait()
 
 
 def write_out(
@@ -518,10 +547,8 @@
             pltpu.VMEM((4, X) + plane, BF16),
             pltpu.SMEM((Y * BLOCKS,), jnp.int32),
             pltpu.SMEM((BLOCKS,), jnp.int32),
-            pltpu.SemaphoreType.DMA((S_H + 19,)),
-            pltpu.SemaphoreType.DMA((S_H + 19,)),
-            pltpu.SemaphoreType.DMA((len(S_WAY),)),
-            pltpu.SemaphoreType.DMA((len(S_WAY),)),
+            pltpu.SemaphoreType.DMA((S_COLUMN + 1,)),
+            pltpu.SemaphoreType.DMA((N_ARRIVE,)),
             pltpu.SemaphoreType.DMA((N_LOCAL,)),
         ],
         compiler_params=pltpu.CompilerParams(

time: 84.2 us -> 78.3 us (0.930)
  Pallas kernels: 83.5 us -> 77.5 us
    pallas_call x1, Pallas kernels: 78.5 us -> 72.5 us  [body(): pl.pallas_call(kernel, out_shape=[jax.ShapeDtypeStruct((4,) + rows, F32),...]
where the time goes in v3:
time: 78.3 us; the launch traced here: 78.1 us
  Pallas kernels  77.5 us (99%)
    pallas_call x1, Pallas kernels, body(): pl.pallas_call(kernel, out_shape=[jax.ShapeDtypeStruct((4,) + rows, F32),...  72.5 us
    pallas_call x1, Pallas kernels, body(): pl.pallas_call(write_out, out_shape=[jax.ShapeDtypeStruct(rows, F32)] * 4...  4.98 us

profile of v3, /device:TPU:1, one launch (start us, length us, event | category | flops | bytes accessed | tf_op | source)
XLA Modules:
  0.0 78.1 jit_solution(13990362113577494752)
XLA Ops:
  0.6 72.5 %shard_map.119 = (f32[4,288,128]{2,1,0:T(8,128)}, bf16[4,8,144,512]{3,2,1,0:T(8,128)(2,1)}) custom-call(bf16[768,4608]{1,0:T(8,128)(2,1)} %bitcast.11, bf16[768,512]{1,0:T(8,128)(2,1)} %bitcast.12, f32[288,128]{1,0:T(8,128)} %bitcast.13, f32[288,128]{1,0:T(8,128)} %bitcast.14, f32[288,128]{1,0:T(8,128)} %bitcast.15, f32[288,128]{1,0:T(8,128)} %bitcast.16, ...), custom_call_target="tpu_custom_call" | custom-call | tf_op jit(solution)/shard_map/pallas_call | solution.py:521
  73.2 5.0 %shard_map.120 = (f32[288,128]{1,0:T(8,128)}, f32[288,128]{1,0:T(8,128)}, f32[288,128]{1,0:T(8,128)}, f32[288,128]{1,0:T(8,128)}, bf16[4,8,144,512]{3,2,1,0:T(8,128)(2,1)}) custom-call(f32[4,288,128]{2,1,0:T(8,128)} %get-tuple-element.12.new_state, bf16[4,8,144,512]{3,2,1,0:T(8,128)(2,1)} %get-tuple-element.13.refreshed), custom_call_target="tpu_custom_call" | custom-call | tf_op jit(solution)/shard_map/pallas_call | solution.py:558

commit v4 on v3

--- a/solution.py
+++ b/solution.py
@@ -147,24 +147,24 @@
 R_SUM = numbered([name for name in sum_steps() if name[0] != "mul" and name not in (("a2", 0), ("b2", "mine"))], 4)
 N_SUM = len(R_SUM)
 R_G = 4 + N_SUM
-R_H = R_G + 7
-R_CROSS = R_H + 7
+R_STATE = R_G + 7
+R_CROSS = R_STATE + 7
 R_WAY = numbered([name + (way,) for name in gather_steps() for way in ways_on(name)], R_CROSS + 12)
 N_ARRIVE = R_CROSS + 12 + len(R_WAY)
-S_CORE, S_SUM, S_G, S_H, S_WAY, S_ROW, S_COLUMN = range(7)
+S_CORE, S_SUM, S_G, S_STATE, S_WAY, S_ROW, S_COLUMN = range(7)
 
 L_ACTS = 0
 L_COT = L_ACTS + 4
 L_STATE = L_COT + 2
 L_NEW = L_STATE + 4
 L_OUT = L_NEW + 1
-N_LOCAL = L_OUT + 24
+N_LOCAL = L_OUT + 1
 
 
 def kernel(
     acts, cot, params, moment1, moment2, ema, live_rows, home, new_state, refreshed,
     acts_buf, cot_buf, own, core_out, core_in, sum_out, sum_in,
-    g_out, g_in, g_all, state, fresh, h_all, h_out, h_in, w_all, w_mine, gathered,
+    g_out, g_in, g_all, g_mine, state, state_out, state_in, fresh, w_mine, gathered,
     position, order, send_sems, recv_sems, local_sems,
 ):
     dp = lax.axis_index("dp")
@@ -211,6 +211,9 @@
         return copy
 
     width = Z * PIECE
+    state_copies = [
+        local(ref, state.at[n], L_STATE + n) for n, ref in enumerate((params, moment1, moment2, ema))
+    ]
     cot_copies = []
     for half in range(2):
         column = pl.multiple_of(256 * lax.rem(c + half, 2), 256)
@@ -220,14 +223,30 @@
     for t, offset in enumerate(OFFSETS):
         column = pl.multiple_of(width * lax.rem(x + offset, X), LANES)
         local(acts.at[:, pl.ds(column, width)], acts_buf.at[t], L_ACTS + t)
-    state_copies = [
-        local(ref, state.at[n], L_STATE + n) for n, ref in enumerate((params, moment1, moment2, ema))
-    ]
+    for copy in state_copies[:3]:
+        copy.wait()
+
+    @pl.loop(0, BLOCKS)
+    def _(i):
+        for n in range(3):
+            for j in range(4):
+                state_out[j // 2, n, j % 2, i] = state[n, pl.ds(i * 32 + j, 8, stride=4), :]
 
     pl.semaphore_wait(barrier, len(greeted))
 
     for copy in cot_copies:
         copy.wait()
+
+    mine = 2 * y + c
+
+    def spread(out, into, group, base):
+        into[mine] = out[c]
+        return [
+            send(out.at[cc], into.at[mine], at(x, z, cc, yy), group, base + n)
+            for n, (cc, yy) in enumerate(others)
+        ]
+
+    state_moves = spread(state_out, state_in, S_STATE, R_STATE)
 
     def core_copy(t):
         return pltpu.make_async_remote_copy(
@@ -235,6 +254,27 @@
             send_sem=send_sems.at[S_CORE], recv_sem=recv_sems.at[R_CORE + t],
             device_id=partner, device_id_type=MESH,
         )
+
+    def read_table():
+        def section_row(s, carry):
+            def block_entry(b, carry):
+                counts, kept = carry[:Y], carry[Y:]
+                keeper = home[s, b]
+                rank = jnp.int32(0)
+                for n in range(Y):
+                    rank = jnp.where(keeper == n, counts[n], rank)
+                place = keeper * BLOCKS + rank
+                position[s * BLOCKS + b] = place
+                counts = tuple(counts[n] + jnp.where(keeper == n, 1, 0) for n in range(Y))
+                here = place - y * BLOCKS
+                kept = tuple(jnp.where(here == n, s * BLOCKS + b, kept[n]) for n in range(BLOCKS))
+                return counts + kept
+
+            return lax.fori_loop(0, BLOCKS, block_entry, carry)
+
+        table = lax.fori_loop(0, Y, section_row, (jnp.int32(0),) * (Y + BLOCKS))
+        for n in range(BLOCKS):
+            order[n] = table[Y + n]
 
     here = {"far": 0, "plus": 1 + c, "minus": 2 - c, "mine": 3}
     needed = {"far": (0,), "plus": (1, 2), "minus": (1, 2), "mine": (3,)}
@@ -301,7 +341,9 @@
     for name in early:
         remember(name, x_next if name[0] == "a1" else along_z(name[2]))
 
-    for name in in_order(sum_steps())[0]:
+    for step, name in enumerate(in_order(sum_steps())[0]):
+        if step == 40:
+            read_table()
         if name[0] == "mul" or name in early:
             continue
         if name[0] == "a1":
@@ -335,98 +377,67 @@
             else:
                 give(name, value, along_x(role))
 
-    mine = 2 * y + c
-
-    def spread(out, into, group, base, meanwhile=None):
-        into[mine] = out[c]
-        copies = []
-        for n, (cc, yy) in enumerate(others):
-            copies.append(
-                send(out.at[cc], into.at[mine], at(x, z, cc, yy), group, base + n)
-            )
-        if meanwhile is not None:
-            meanwhile()
-        for copy in copies:
-            copy.wait_recv()
-
-    def read_table():
-        def section_row(s, carry):
-            def block_entry(b, carry):
-                counts, kept = carry[:Y], carry[Y:]
-                keeper = home[s, b]
-                rank = jnp.int32(0)
-                for n in range(Y):
-                    rank = jnp.where(keeper == n, counts[n], rank)
-                place = keeper * BLOCKS + rank
-                position[s * BLOCKS + b] = place
-                counts = tuple(counts[n] + jnp.where(keeper == n, 1, 0) for n in range(Y))
-                here = place - y * BLOCKS
-                kept = tuple(jnp.where(here == n, s * BLOCKS + b, kept[n]) for n in range(BLOCKS))
-                return counts + kept
-
-            return lax.fori_loop(0, BLOCKS, block_entry, carry)
-
-        table = lax.fori_loop(0, Y, section_row, (jnp.int32(0),) * (Y + BLOCKS))
-        for n in range(BLOCKS):
-            order[n] = table[Y + n]
-
     for cc in range(2):
         rows = slice(HALF * cc, HALF * (cc + 1))
         g_out[cc] = jnp.concatenate([sum_a[rows], sum_b[rows]], axis=0).astype(BF16)
-    spread(g_out, g_in, S_G, R_G, read_table)
-    for s in range(Y):
-        for cc in range(2):
-            value = g_in[2 * s + cc].astype(F32)
-            for jj in range(2):
-                g_all[2 * cc + jj, BLOCKS * s : BLOCKS * (s + 1)] = value[HALF * jj : HALF * (jj + 1)].reshape(
-                    BLOCKS, 8, LANES
-                )
-
-    for copy in state_copies:
-        copy.wait()
+    gradient_moves = spread(g_out, g_in, S_G, R_G)
+
     corr_one = 1.0 - 0.9**STEP
     corr_two = 1.0 - 0.99**STEP
-
-    @pl.loop(0, BLOCKS)
-    def _(i):
-        f = order[i]
-        s = lax.div(f, BLOCKS)
-        b = f - s * BLOCKS
-        limit = live_rows[s] - (dp * (4 * HALF) + b * 32)
-        tile = lax.broadcasted_iota(jnp.int32, (8, LANES), 0)
-        generator = tile * 0 + s < N_GEN
-        for j in range(4):
-            rows = pl.ds(i * 32 + j, 8, stride=4)
-            grads = g_all[j, f]
-            alive = tile * 4 + j < limit
-            p, m1, m2, average = (state[n, rows, :] for n in range(4))
-            first = jnp.where(alive, 0.9 * m1 + 0.1 * grads, m1)
-            second = jnp.where(alive, 0.99 * m2 + 0.01 * grads * grads, m2)
-            stepped = p - 0.0025 * (first / corr_one) / (jnp.sqrt(second / corr_two) + 1e-08)
-            updated = jnp.where(alive, stepped, p)
-            averaged = jnp.where(generator, 0.995 * average + 0.005 * updated, average)
-            for n, value in enumerate((updated, first, second, averaged)):
-                fresh[n, rows, :] = value
-            h_all[j, pl.ds(pl.multiple_of(i * 8, 8), 8), :] = updated
-
-    for cc in range(2):
-        h_out[cc] = h_all[2 * cc : 2 * cc + 2].reshape(PIECE, LANES).astype(BF16)
-    spread(h_out, h_in, S_H, R_H)
-    fresh_copy = local(fresh, new_state, L_NEW)
-    for s in range(Y):
-        for cc in range(2):
-            value = h_in[2 * s + cc].astype(F32)
-            for jj in range(2):
-                w_all[jj, cc, BLOCKS * s : BLOCKS * (s + 1)] = value[HALF * jj : HALF * (jj + 1)].reshape(
-                    BLOCKS, 8, LANES
-                )
+    tile = lax.broadcasted_iota(jnp.int32, (8, LANES), 0)
+
+    def adam(p, m1, m2, grads, alive):
+        first = jnp.where(alive, 0.9 * m1 + 0.1 * grads, m1)
+        second = jnp.where(alive, 0.99 * m2 + 0.01 * grads * grads, m2)
+        stepped = p - 0.0025 * (first / corr_one) / (jnp.sqrt(second / corr_two) + 1e-08)
+        return jnp.where(alive, stepped, p), first, second
+
+    for jj, value in enumerate((sum_a, sum_b)):
+        g_mine[jj] = value.astype(BF16).astype(F32).reshape(2, BLOCKS, 8, LANES)
+    for copy in state_moves:
+        copy.wait_recv()
 
     @pl.loop(0, BLOCKS)
     def _(b):
         place = position[y * BLOCKS + b]
+        keeper = lax.div(place, BLOCKS)
+        rank = place - keeper * BLOCKS
         for cc in range(2):
+            limit = live_rows[y] - ((dp - c + cc) * (4 * HALF) + b * 32)
             for jj in range(2):
-                w_mine[jj, pl.ds(pl.multiple_of(HALF * cc + b * 8, 8), 8), :] = w_all[jj, cc, place]
+                alive = tile * 4 + (2 * c + jj) < limit
+                p, m1, m2 = (state_in[2 * keeper + cc, n, jj, rank] for n in range(3))
+                updated, _, _ = adam(p, m1, m2, g_mine[jj, cc, b], alive)
+                w_mine[jj, pl.ds(pl.multiple_of(HALF * cc + b * 8, 8), 8), :] = updated
+
+    def update_kept():
+        for copy in gradient_moves:
+            copy.wait_recv()
+        state_copies[3].wait()
+        for s in range(Y):
+            for cc in range(2):
+                value = g_in[2 * s + cc].astype(F32)
+                for jj in range(2):
+                    rows = value[HALF * jj : HALF * (jj + 1)]
+                    g_all[2 * cc + jj, BLOCKS * s : BLOCKS * (s + 1)] = rows.reshape(BLOCKS, 8, LANES)
+
+        @pl.loop(0, BLOCKS)
+        def _(i):
+            f = order[i]
+            s = lax.div(f, BLOCKS)
+            b = f - s * BLOCKS
+            limit = live_rows[s] - (dp * (4 * HALF) + b * 32)
+            generator = tile * 0 + s < N_GEN
+            for j in range(4):
+                rows = pl.ds(i * 32 + j, 8, stride=4)
+                alive = tile * 4 + j < limit
+                p, m1, m2, average = (state[n, rows, :] for n in range(4))
+                updated, first, second = adam(p, m1, m2, g_all[j, f], alive)
+                averaged = jnp.where(generator, 0.995 * average + 0.005 * updated, average)
+                for n, value in enumerate((updated, first, second, averaged)):
+                    fresh[n, rows, :] = value
+
+        return local(fresh, new_state, L_NEW)
 
     ja, jb = 2 * c, 2 * c + 1
     gathered[ja, x, z] = w_mine[0].astype(BF16)
@@ -444,7 +455,7 @@
         at_sender = (name[0], back, name[2]) if axis == "x" else (name[0], name[1], back)
         moving[at_sender + (axis + ("_next" if i < 0 else "_last"),)].wait_recv()
 
-    seen, crossing, written = [], {}, []
+    seen, crossing = [], {}
 
     def write(j, xx, zz):
         lanes = pl.ds(pl.multiple_of(j * LANES, LANES), LANES)
@@ -452,7 +463,7 @@
             source, target = gathered.at[j, xx], refreshed.at[xx, :, :, lanes]
         else:
             source, target = gathered.at[j, :, zz], refreshed.at[:, zz, :, lanes]
-        written.append(local(source, target, L_OUT + len(written)))
+        local(source, target, L_OUT)
 
     def cross(half, i, k):
         number = len(crossing)
@@ -460,7 +471,9 @@
         ref = gathered.at[halves[half], xi(i)] if half == "wa" else gathered.at[halves[half], :, zi(k)]
         crossing[half, i, k] = send(ref, ref, partner, S_ROW if half == "wa" else S_COLUMN, R_CROSS + number)
 
-    for name in in_order(gather_steps())[0]:
+    for step, name in enumerate(in_order(gather_steps())[0]):
+        if step == 44:
+            fresh_copy = update_kept()
         half, i, k = name
         first, second = (("z", k), ("x", i)) if half == "wa" else (("x", i), ("z", k))
         if second[1] != 0:
@@ -478,12 +491,11 @@
     for (half, i, k), copy in crossing.items():
         copy.wait_recv()
         write(2 * (1 - c) + (half == "wb"), None if half == "wb" else xi(-i), zi(-k))
-    for copy in written:
-        copy.wait()
+    pltpu.make_async_copy(gathered, gathered, local_sems.at[L_OUT]).wait()
     fresh_copy.wait()
 
     for group, ref in (
-        (S_CORE, core_out), (S_SUM, sum_out), (S_G, g_in.at[pl.ds(0, 7)]), (S_H, h_in.at[pl.ds(0, 7)]),
+        (S_CORE, core_out), (S_SUM, sum_out), (S_G, g_in.at[pl.ds(0, 7)]), (S_STATE, state_in.at[pl.ds(0, 7)]),
         (S_WAY, sum_out), (S_ROW, gathered.at[0]), (S_COLUMN, gathered.at[0]),
     ):
         pltpu.make_async_copy(ref, ref, send_sems.at[group]).wait()
@@ -537,12 +549,11 @@
             pltpu.VMEM((2,) + chunk, BF16),
             pltpu.VMEM((2 * Y,) + chunk, BF16),
             pltpu.VMEM((4, Y * BLOCKS, 8, LANES), F32),
+            pltpu.VMEM((2, 2, BLOCKS, 8, LANES), F32),
             pltpu.VMEM((4,) + rows, F32),
+            pltpu.VMEM((2, 3, 2, BLOCKS, 8, LANES), F32),
+            pltpu.VMEM((2 * Y, 3, 2, BLOCKS, 8, LANES), F32),
             pltpu.VMEM((4,) + rows, F32),
-            pltpu.VMEM((4, HALF, LANES), F32),
-            pltpu.VMEM((2,) + chunk, BF16),
-            pltpu.VMEM((2 * Y,) + chunk, BF16),
-            pltpu.VMEM((2, 2, Y * BLOCKS, 8, LANES), F32),
             pltpu.VMEM((2,) + chunk, F32),
             pltpu.VMEM((4, X) + plane, BF16),
             pltpu.SMEM((Y * BLOCKS,), jnp.int32),

time: 78.3 us -> 69 us (0.88)
  Pallas kernels: 77.5 us -> 68.2 us
    pallas_call x1, Pallas kernels: 72.5 us -> 63.3 us  [body(): pl.pallas_call(kernel, out_shape=[jax.ShapeDtypeStruct((4,) + rows, F32),...]
where the time goes in v4:
time: 69 us; the launch traced here: 68.9 us
  Pallas kernels  68.2 us (99%)
    pallas_call x1, Pallas kernels, body(): pl.pallas_call(kernel, out_shape=[jax.ShapeDtypeStruct((4,) + rows, F32),...  63.3 us
    pallas_call x1, Pallas kernels, body(): pl.pallas_call(write_out, out_shape=[jax.ShapeDtypeStruct(rows, F32)] * 4...  4.98 us

profile of v4, /device:TPU:1, one launch (start us, length us, event | category | flops | bytes accessed | tf_op | source)
XLA Modules:
  0.0 68.9 jit_solution(12515308572408357332)
XLA Ops:
  0.6 63.3 %shard_map.119 = (f32[4,288,128]{2,1,0:T(8,128)}, bf16[4,8,144,512]{3,2,1,0:T(8,128)(2,1)}) custom-call(bf16[768,4608]{1,0:T(8,128)(2,1)} %bitcast.11, bf16[768,512]{1,0:T(8,128)(2,1)} %bitcast.12, f32[288,128]{1,0:T(8,128)} %bitcast.13, f32[288,128]{1,0:T(8,128)} %bitcast.14, f32[288,128]{1,0:T(8,128)} %bitcast.15, f32[288,128]{1,0:T(8,128)} %bitcast.16, ...), custom_call_target="tpu_custom_call" | custom-call | tf_op jit(solution)/shard_map/pallas_call | solution.py:533
  63.9 5.0 %shard_map.120 = (f32[288,128]{1,0:T(8,128)}, f32[288,128]{1,0:T(8,128)}, f32[288,128]{1,0:T(8,128)}, f32[288,128]{1,0:T(8,128)}, bf16[4,8,144,512]{3,2,1,0:T(8,128)(2,1)}) custom-call(f32[4,288,128]{2,1,0:T(8,128)} %get-tuple-element.12.new_state, bf16[4,8,144,512]{3,2,1,0:T(8,128)(2,1)} %get-tuple-element.13.refreshed), custom_call_target="tpu_custom_call" | custom-call | tf_op jit(solution)/shard_map/pallas_call | solution.py:569

commit v5 on v4

--- a/solution.py
+++ b/solution.py
@@ -149,22 +149,20 @@
 R_G = 4 + N_SUM
 R_STATE = R_G + 7
 R_CROSS = R_STATE + 7
-R_WAY = numbered([name + (way,) for name in gather_steps() for way in ways_on(name)], R_CROSS + 12)
-N_ARRIVE = R_CROSS + 12 + len(R_WAY)
-S_CORE, S_SUM, S_G, S_STATE, S_WAY, S_ROW, S_COLUMN = range(7)
+R_WAY = numbered([name + (way,) for name in gather_steps() for way in ways_on(name)], R_CROSS + 2 * Z)
+N_ARRIVE = R_CROSS + 2 * Z + len(R_WAY)
+S_CORE, S_SUM, S_G, S_STATE, S_WAY, S_CROSS = range(6)
 
 L_ACTS = 0
 L_COT = L_ACTS + 4
 L_STATE = L_COT + 2
-L_NEW = L_STATE + 4
-L_OUT = L_NEW + 1
-N_LOCAL = L_OUT + 1
+N_LOCAL = L_STATE + 4
 
 
 def kernel(
-    acts, cot, params, moment1, moment2, ema, live_rows, home, new_state, refreshed,
+    acts, cot, params, moment1, moment2, ema, live_rows, home, fresh, gathered,
     acts_buf, cot_buf, own, core_out, core_in, sum_out, sum_in,
-    g_out, g_in, g_all, g_mine, state, state_out, state_in, fresh, w_mine, gathered,
+    g_out, g_in, g_all, g_mine, state, state_out, state_in, w_mine,
     position, order, send_sems, recv_sems, local_sems,
 ):
     dp = lax.axis_index("dp")
@@ -437,8 +435,6 @@
                 for n, value in enumerate((updated, first, second, averaged)):
                     fresh[n, rows, :] = value
 
-        return local(fresh, new_state, L_NEW)
-
     ja, jb = 2 * c, 2 * c + 1
     gathered[ja, x, z] = w_mine[0].astype(BF16)
     gathered[jb, x, z] = w_mine[1].astype(BF16)
@@ -457,23 +453,16 @@
 
     seen, crossing = [], {}
 
-    def write(j, xx, zz):
-        lanes = pl.ds(pl.multiple_of(j * LANES, LANES), LANES)
-        if xx is not None:
-            source, target = gathered.at[j, xx], refreshed.at[xx, :, :, lanes]
-        else:
-            source, target = gathered.at[j, :, zz], refreshed.at[:, zz, :, lanes]
-        local(source, target, L_OUT)
-
-    def cross(half, i, k):
-        number = len(crossing)
-        write(halves[half], None if half == "wb" else xi(i), zi(k))
-        ref = gathered.at[halves[half], xi(i)] if half == "wa" else gathered.at[halves[half], :, zi(k)]
-        crossing[half, i, k] = send(ref, ref, partner, S_ROW if half == "wa" else S_COLUMN, R_CROSS + number)
+    def cross(half, k):
+        ref = gathered.at[halves[half], :, zi(k)]
+        crossing[half, k] = send(ref, ref, partner, S_CROSS, R_CROSS + len(crossing))
+
+    def crossed_over(half, k):
+        crossing[half, k].wait_recv()
 
     for step, name in enumerate(in_order(gather_steps())[0]):
         if step == 44:
-            fresh_copy = update_kept()
+            update_kept()
         half, i, k = name
         first, second = (("z", k), ("x", i)) if half == "wa" else (("x", i), ("z", k))
         if second[1] != 0:
@@ -483,43 +472,28 @@
         for way in ways_on(name):
             go(name, way)
         seen.append(name)
-        if half == "wa" and sum(n[:2] == name[:2] for n in seen) == Z:
-            cross("wa", i, 0)
-        if half == "wb" and sum(n[0] == "wb" and n[2] == k for n in seen) == X:
-            cross("wb", 0, k)
-
-    for (half, i, k), copy in crossing.items():
-        copy.wait_recv()
-        write(2 * (1 - c) + (half == "wb"), None if half == "wb" else xi(-i), zi(-k))
-    pltpu.make_async_copy(gathered, gathered, local_sems.at[L_OUT]).wait()
-    fresh_copy.wait()
+        if sum(n[0] == half and n[2] == k for n in seen) == X:
+            cross(half, k)
+
+    for column in crossing:
+        crossed_over(*column)
 
     for group, ref in (
         (S_CORE, core_out), (S_SUM, sum_out), (S_G, g_in.at[pl.ds(0, 7)]), (S_STATE, state_in.at[pl.ds(0, 7)]),
-        (S_WAY, sum_out), (S_ROW, gathered.at[0]), (S_COLUMN, gathered.at[0]),
+        (S_WAY, sum_out), (S_CROSS, gathered.at[pl.ds(0, 2)]),
     ):
         pltpu.make_async_copy(ref, ref, send_sems.at[group]).wait()
 
 
-def write_out(
-    new_state, refreshed, new_params, new_moment1, new_moment2, new_ema, weights, state_buf, buf, in_sems, out_sems
-):
+def write_out(fresh, gathered, new_params, new_moment1, new_moment2, new_ema, weights, sems):
     moves = [
-        (new_state.at[n], state_buf.at[n], ref)
-        for n, ref in enumerate((new_params, new_moment1, new_moment2, new_ema))
+        (gathered.at[j, xx], weights.at[xx, :, :, pl.ds(LANES * j, LANES)]) for xx in range(X) for j in range(4)
     ]
-    for xx in range(X):
-        for half in range(2):
-            part = pl.ds(4 * half, 4)
-            moves.append((refreshed.at[xx, part], buf.at[xx, part], weights.at[xx, part]))
-    first = [pltpu.make_async_copy(a, b, in_sems.at[n]) for n, (a, b, _) in enumerate(moves)]
-    second = [pltpu.make_async_copy(b, d, out_sems.at[n]) for n, (_, b, d) in enumerate(moves)]
-    for copy in first:
+    moves += [(fresh.at[n], ref) for n, ref in enumerate((new_params, new_moment1, new_moment2, new_ema))]
+    copies = [pltpu.make_async_copy(source, target, sems.at[n]) for n, (source, target) in enumerate(moves)]
+    for copy in copies:
         copy.start()
-    for arrived, copy in zip(first, second):
-        arrived.wait()
-        copy.start()
-    for copy in second:
+    for copy in copies:
         copy.wait()
 
 
@@ -533,11 +507,11 @@
     outs = pl.pallas_call(
         kernel,
         out_shape=[
-            jax.ShapeDtypeStruct((4,) + rows, F32),
-            jax.ShapeDtypeStruct((X, Z, PIECE, 4 * LANES), BF16),
+            pltpu.VMEM((4,) + rows, F32),
+            pltpu.VMEM((4, X) + plane, BF16),
         ],
         in_specs=[any_space] * 6 + [smem] * 2,
-        out_specs=[any_space] * 2,
+        out_specs=[pl.BlockSpec(memory_space=pltpu.VMEM)] * 2,
         scratch_shapes=[
             pltpu.VMEM((X, tokens, Z * PIECE), BF16),
             pltpu.VMEM((tokens, 4 * LANES), BF16),
@@ -553,32 +527,27 @@
             pltpu.VMEM((4,) + rows, F32),
             pltpu.VMEM((2, 3, 2, BLOCKS, 8, LANES), F32),
             pltpu.VMEM((2 * Y, 3, 2, BLOCKS, 8, LANES), F32),
-            pltpu.VMEM((4,) + rows, F32),
             pltpu.VMEM((2,) + chunk, F32),
-            pltpu.VMEM((4, X) + plane, BF16),
             pltpu.SMEM((Y * BLOCKS,), jnp.int32),
             pltpu.SMEM((BLOCKS,), jnp.int32),
-            pltpu.SemaphoreType.DMA((S_COLUMN + 1,)),
+            pltpu.SemaphoreType.DMA((S_CROSS + 1,)),
             pltpu.SemaphoreType.DMA((N_ARRIVE,)),
             pltpu.SemaphoreType.DMA((N_LOCAL,)),
         ],
         compiler_params=pltpu.CompilerParams(
-            collective_id=0, has_side_effects=True, vmem_limit_bytes=56 * 2**20
+            collective_id=0, has_side_effects=True, vmem_limit_bytes=57 * 2**20
         ),
     )(acts[0], grad_out[0], params[0], moment1[0], moment2[0], ema[0], live_rows, home)
     updated, first, second, averaged, weights = pl.pallas_call(
         write_out,
         out_shape=[jax.ShapeDtypeStruct(rows, F32)] * 4
         + [jax.ShapeDtypeStruct((X, Z, PIECE, 4 * LANES), BF16)],
-        in_specs=[any_space] * 2,
+        in_specs=[pl.BlockSpec(memory_space=pltpu.VMEM)] * 2,
         out_specs=[any_space] * 5,
         scratch_shapes=[
-            pltpu.VMEM((4,) + rows, F32),
-            pltpu.VMEM((X, Z, PIECE, 4 * LANES), BF16),
-            pltpu.SemaphoreType.DMA((4 + 2 * X,)),
-            pltpu.SemaphoreType.DMA((4 + 2 * X,)),
+            pltpu.SemaphoreType.DMA((4 * X + 4,)),
         ],
-        compiler_params=pltpu.CompilerParams(vmem_limit_bytes=56 * 2**20),
+        compiler_params=pltpu.CompilerParams(vmem_limit_bytes=40 * 2**20),
     )(*outs)
     return (
         updated[None], first[None], second[None], averaged[None],

time: 69 us -> 65.9 us (0.955)
  Pallas kernels: 68.2 us -> 65.1 us
    pallas_call x1, Pallas kernels: 4.98 us -> 2.52 us  [body(): pl.pallas_call(write_out, out_shape=[jax.ShapeDtypeStruct(rows, F32)] * 4...]
where the time goes in v5:
time: 65.9 us; the launch traced here: 65.8 us
  Pallas kernels  65.1 us (99%)
    pallas_call x1, Pallas kernels, body(): pl.pallas_call(kernel, out_shape=[pltpu.VMEM((4,) + rows, F32), pltpu.VME...  62.6 us
    pallas_call x1, Pallas kernels, body(): pl.pallas_call(write_out, out_shape=[jax.ShapeDtypeStruct(rows, F32)] * 4...  2.52 us

profile of v5, /device:TPU:1, one launch (start us, length us, event | category | flops | bytes accessed | tf_op | source)
XLA Modules:
  0.0 65.8 jit_solution(7740641249269855964)
XLA Ops:
  0.6 62.6 %shard_map.119 = (f32[4,288,128]{2,1,0:T(8,128)S(1)}, bf16[4,4,8,144,128]{4,3,2,1,0:T(8,128)(2,1)S(1)}) custom-call(bf16[768,4608]{1,0:T(8,128)(2,1)} %bitcast.11, bf16[768,512]{1,0:T(8,128)(2,1)} %bitcast.12, f32[288,128]{1,0:T(8,128)} %bitcast.13, f32[288,128]{1,0:T(8,128)} %bitcast.14, f32[288,128]{1,0:T(8,128)} %bitcast.15, f32[288,128]{1,0:T(8,128)} %bitcast.16, ...), custom_call_target="tpu_custom_call" | custom-call | tf_op jit(solution)/shard_map/pallas_call | solution.py:507
  63.2 2.5 %shard_map.120 = (f32[288,128]{1,0:T(8,128)}, f32[288,128]{1,0:T(8,128)}, f32[288,128]{1,0:T(8,128)}, f32[288,128]{1,0:T(8,128)}, bf16[4,8,144,512]{3,2,1,0:T(8,128)(2,1)}) custom-call(f32[4,288,128]{2,1,0:T(8,128)S(1)} %get-tuple-element.12.fresh, bf16[4,4,8,144,128]{4,3,2,1,0:T(8,128)(2,1)S(1)} %get-tuple-element.13.gathered), custom_call_target="tpu_custom_call" | custom-call | tf_op jit(solution)/shard_map/pallas_call | solution.py:541

commit v6 on v5

--- a/solution.py
+++ b/solution.py
@@ -17,7 +17,7 @@
 BLOCKS = 9
 OFFSETS = (2, 1, 3, 0)
 
-LATENCY, PIECE_US, STEP_US = 2.2, 0.39, 0.12
+LATENCY, PIECE_US, STEP_US = 1.7, 0.39, 0.4
 
 
 def in_order(steps):
@@ -162,7 +162,7 @@
 def kernel(
     acts, cot, params, moment1, moment2, ema, live_rows, home, fresh, gathered,
     acts_buf, cot_buf, own, core_out, core_in, sum_out, sum_in,
-    g_out, g_in, g_all, g_mine, state, state_out, state_in, w_mine,
+    g_out, g_in, g_all, state, state_out, state_in, state_mine,
     position, order, send_sems, recv_sems, local_sems,
 ):
     dp = lax.axis_index("dp")
@@ -209,18 +209,23 @@
         return copy
 
     width = Z * PIECE
-    state_copies = [
-        local(ref, state.at[n], L_STATE + n) for n, ref in enumerate((params, moment1, moment2, ema))
-    ]
     cot_copies = []
     for half in range(2):
         column = pl.multiple_of(256 * lax.rem(c + half, 2), 256)
         cot_copies.append(
             local(cot.at[:, pl.ds(column, 256)], cot_buf.at[:, pl.ds(256 * half, 256)], L_COT + half)
         )
-    for t, offset in enumerate(OFFSETS):
+
+    def load_acts(t, offset):
         column = pl.multiple_of(width * lax.rem(x + offset, X), LANES)
         local(acts.at[:, pl.ds(column, width)], acts_buf.at[t], L_ACTS + t)
+
+    load_acts(0, OFFSETS[0])
+    state_copies = [
+        local(ref, state.at[n], L_STATE + n) for n, ref in enumerate((params, moment1, moment2, ema))
+    ]
+    load_acts(1, OFFSETS[1])
+
     for copy in state_copies[:3]:
         copy.wait()
 
@@ -318,6 +323,11 @@
         pltpu.make_async_copy(
             acts.at[:, pl.ds(0, width)], acts_buf.at[t], local_sems.at[L_ACTS + t]
         ).wait()
+
+        @pl.when(t < X - 2)
+        def _():
+            load_acts(t + 2, lax.select(t == 0, OFFSETS[2], OFFSETS[3]))
+
         product = lax.dot_general(
             acts_buf[t], cot_buf[...], (((0,), (0,)), ((), ())), preferred_element_type=F32
         )
@@ -339,9 +349,25 @@
     for name in early:
         remember(name, x_next if name[0] == "a1" else along_z(name[2]))
 
+    def collect():
+        for copy in state_moves:
+            copy.wait_recv()
+
+        @pl.loop(0, BLOCKS)
+        def _(b):
+            place = position[y * BLOCKS + b]
+            keeper = lax.div(place, BLOCKS)
+            rank = place - keeper * BLOCKS
+            for cc in range(2):
+                for n in range(3):
+                    for jj in range(2):
+                        state_mine[n, jj, cc, b] = state_in[2 * keeper + cc, n, jj, rank]
+
     for step, name in enumerate(in_order(sum_steps())[0]):
         if step == 40:
             read_table()
+        if step == len(sum_steps()) - 3:
+            collect()
         if name[0] == "mul" or name in early:
             continue
         if name[0] == "a1":
@@ -375,11 +401,6 @@
             else:
                 give(name, value, along_x(role))
 
-    for cc in range(2):
-        rows = slice(HALF * cc, HALF * (cc + 1))
-        g_out[cc] = jnp.concatenate([sum_a[rows], sum_b[rows]], axis=0).astype(BF16)
-    gradient_moves = spread(g_out, g_in, S_G, R_G)
-
     corr_one = 1.0 - 0.9**STEP
     corr_two = 1.0 - 0.99**STEP
     tile = lax.broadcasted_iota(jnp.int32, (8, LANES), 0)
@@ -390,25 +411,21 @@
         stepped = p - 0.0025 * (first / corr_one) / (jnp.sqrt(second / corr_two) + 1e-08)
         return jnp.where(alive, stepped, p), first, second
 
-    for jj, value in enumerate((sum_a, sum_b)):
-        g_mine[jj] = value.astype(BF16).astype(F32).reshape(2, BLOCKS, 8, LANES)
-    for copy in state_moves:
-        copy.wait_recv()
-
-    @pl.loop(0, BLOCKS)
-    def _(b):
-        place = position[y * BLOCKS + b]
-        keeper = lax.div(place, BLOCKS)
-        rank = place - keeper * BLOCKS
+    sums = [value.astype(BF16).astype(F32) for value in (sum_a, sum_b)]
+    limit = live_rows[y] - (dp - c) * (4 * HALF)
+    row = lax.broadcasted_iota(jnp.int32, (PIECE, LANES), 0) * 4
+    for jj in range(2):
+        p, m1, m2 = (state_mine[n, jj].reshape(PIECE, LANES) for n in range(3))
+        updated, _, _ = adam(p, m1, m2, sums[jj], row + (2 * c + jj) < limit)
+        gathered[2 * c + jj, x, z] = updated.astype(BF16)
+
+    def send_gradient():
         for cc in range(2):
-            limit = live_rows[y] - ((dp - c + cc) * (4 * HALF) + b * 32)
-            for jj in range(2):
-                alive = tile * 4 + (2 * c + jj) < limit
-                p, m1, m2 = (state_in[2 * keeper + cc, n, jj, rank] for n in range(3))
-                updated, _, _ = adam(p, m1, m2, g_mine[jj, cc, b], alive)
-                w_mine[jj, pl.ds(pl.multiple_of(HALF * cc + b * 8, 8), 8), :] = updated
-
-    def update_kept():
+            rows = slice(HALF * cc, HALF * (cc + 1))
+            g_out[cc] = jnp.concatenate([value[rows] for value in sums], axis=0).astype(BF16)
+        return spread(g_out, g_in, S_G, R_G)
+
+    def update_kept(gradient_moves):
         for copy in gradient_moves:
             copy.wait_recv()
         state_copies[3].wait()
@@ -436,8 +453,6 @@
                     fresh[n, rows, :] = value
 
     ja, jb = 2 * c, 2 * c + 1
-    gathered[ja, x, z] = w_mine[0].astype(BF16)
-    gathered[jb, x, z] = w_mine[1].astype(BF16)
     halves = {"wa": ja, "wb": jb}
     ways = {"z_next": z_next, "z_last": z_last, "x_next": x_next, "x_last": x_last}
 
@@ -460,9 +475,13 @@
     def crossed_over(half, k):
         crossing[half, k].wait_recv()
 
-    for step, name in enumerate(in_order(gather_steps())[0]):
-        if step == 44:
-            update_kept()
+    gather_order = in_order(gather_steps())[0]
+    last_sent = max(step for step, name in enumerate(gather_order) if ways_on(name))
+    for step, name in enumerate(gather_order):
+        if step == 6:
+            gradient_moves = send_gradient()
+        if step == last_sent + 1:
+            update_kept(gradient_moves)
         half, i, k = name
         first, second = (("z", k), ("x", i)) if half == "wa" else (("x", i), ("z", k))
         if second[1] != 0:
@@ -523,11 +542,10 @@
             pltpu.VMEM((2,) + chunk, BF16),
             pltpu.VMEM((2 * Y,) + chunk, BF16),
             pltpu.VMEM((4, Y * BLOCKS, 8, LANES), F32),
-            pltpu.VMEM((2, 2, BLOCKS, 8, LANES), F32),
             pltpu.VMEM((4,) + rows, F32),
             pltpu.VMEM((2, 3, 2, BLOCKS, 8, LANES), F32),
             pltpu.VMEM((2 * Y, 3, 2, BLOCKS, 8, LANES), F32),
-            pltpu.VMEM((2,) + chunk, F32),
+            pltpu.VMEM((3, 2, 2, BLOCKS, 8, LANES), F32),
             pltpu.SMEM((Y * BLOCKS,), jnp.int32),
             pltpu.SMEM((BLOCKS,), jnp.int32),
             pltpu.SemaphoreType.DMA((S_CROSS + 1,)),

time: 65.9 us -> 62.6 us (0.950)
  Pallas kernels: 65.1 us -> 61.9 us
    pallas_call x1, Pallas kernels: 62.6 us -> 59.3 us  [body(): pl.pallas_call(kernel, out_shape=[pltpu.VMEM((4,) + rows, F32), pltpu.VME...]
where the time goes in v6:
time: 62.6 us; the launch traced here: 62.5 us
  Pallas kernels  61.9 us (99%)
  between operations  0.64 us (1%)
    pallas_call x1, Pallas kernels, body(): pl.pallas_call(kernel, out_shape=[pltpu.VMEM((4,) + rows, F32), pltpu.VME...  59.3 us
    pallas_call x1, Pallas kernels, body(): pl.pallas_call(write_out, out_shape=[jax.ShapeDtypeStruct(rows, F32)] * 4...  2.52 us

profile of v6, /device:TPU:1, one launch (start us, length us, event | category | flops | bytes accessed | tf_op | source)
XLA Modules:
  0.0 62.5 jit_solution(1044891748847056573)
XLA Ops:
  0.6 59.3 %shard_map.119 = (f32[4,288,128]{2,1,0:T(8,128)S(1)}, bf16[4,4,8,144,128]{4,3,2,1,0:T(8,128)(2,1)S(1)}) custom-call(bf16[768,4608]{1,0:T(8,128)(2,1)} %bitcast.11, bf16[768,512]{1,0:T(8,128)(2,1)} %bitcast.12, f32[288,128]{1,0:T(8,128)} %bitcast.13, f32[288,128]{1,0:T(8,128)} %bitcast.14, f32[288,128]{1,0:T(8,128)} %bitcast.15, f32[288,128]{1,0:T(8,128)} %bitcast.16, ...), custom_call_target="tpu_custom_call" | custom-call | tf_op jit(solution)/shard_map/pallas_call | solution.py:526
  60.0 2.5 %shard_map.120 = (f32[288,128]{1,0:T(8,128)}, f32[288,128]{1,0:T(8,128)}, f32[288,128]{1,0:T(8,128)}, f32[288,128]{1,0:T(8,128)}, bf16[4,8,144,512]{3,2,1,0:T(8,128)(2,1)}) custom-call(f32[4,288,128]{2,1,0:T(8,128)S(1)} %get-tuple-element.12.fresh, bf16[4,4,8,144,128]{4,3,2,1,0:T(8,128)(2,1)S(1)} %get-tuple-element.13.gathered), custom_call_target="tpu_custom_call" | custom-call | tf_op jit(solution)/shard_map/pallas_call | solution.py:559

commit v7 on v6

--- a/solution.py
+++ b/solution.py
@@ -316,7 +316,7 @@
     def along_z(k):
         return z_next if k > 0 else z_last
 
-    early = [("a1", "far", k) for k in CHAIN + (0,)] + [("b1", "far", 4), ("b1", "far", -3)]
+    early = [("b1", "far", 4), ("b1", "far", -3)] + [("a1", "far", k) for k in CHAIN + (0,)]
 
     @pl.loop(0, X)
     def _(t):
@@ -337,14 +337,21 @@
             core_out[t, h] = other.reshape(Z, PIECE, LANES).astype(BF16)
         core_copy(t).start()
 
-        @pl.when(t == 1)
-        def _():
-            core_copy(0).wait_recv()
-            for name in early:
+        def send_early(names):
+            for name in names:
                 half, role, k = name
                 value = block(0 if half == "a1" else 1, role, k)
                 sum_out[R_SUM[name] - 4] = value.astype(BF16)
                 piece_copy(name, x_next if half == "a1" else along_z(k)).start()
+
+        @pl.when(t == 1)
+        def _():
+            core_copy(0).wait_recv()
+            send_early(early[:6])
+
+        @pl.when(t == 2)
+        def _():
+            send_early(early[6:])
 
     for name in early:
         remember(name, x_next if name[0] == "a1" else along_z(name[2]))

time: 62.6 us -> 62.7 us (level)
  no operation moved by 1% of the time
where the time goes in v7:
time: 62.7 us; the launch traced here: 62.5 us
  Pallas kernels  61.9 us (99%)
  between operations  0.64 us (1%)
    pallas_call x1, Pallas kernels, body(): pl.pallas_call(kernel, out_shape=[pltpu.VMEM((4,) + rows, F32), pltpu.VME...  59.4 us
    pallas_call x1, Pallas kernels, body(): pl.pallas_call(write_out, out_shape=[jax.ShapeDtypeStruct(rows, F32)] * 4...  2.52 us

profile of v7, /device:TPU:1, one launch (start us, length us, event | category | flops | bytes accessed | tf_op | source)
XLA Modules:
  0.0 62.5 jit_solution(8226133049265255644)
XLA Ops:
  0.6 59.4 %shard_map.119 = (f32[4,288,128]{2,1,0:T(8,128)S(1)}, bf16[4,4,8,144,128]{4,3,2,1,0:T(8,128)(2,1)S(1)}) custom-call(bf16[768,4608]{1,0:T(8,128)(2,1)} %bitcast.11, bf16[768,512]{1,0:T(8,128)(2,1)} %bitcast.12, f32[288,128]{1,0:T(8,128)} %bitcast.13, f32[288,128]{1,0:T(8,128)} %bitcast.14, f32[288,128]{1,0:T(8,128)} %bitcast.15, f32[288,128]{1,0:T(8,128)} %bitcast.16, ...), custom_call_target="tpu_custom_call" | custom-call | tf_op jit(solution)/shard_map/pallas_call | solution.py:533
  60.0 2.5 %shard_map.120 = (f32[288,128]{1,0:T(8,128)}, f32[288,128]{1,0:T(8,128)}, f32[288,128]{1,0:T(8,128)}, f32[288,128]{1,0:T(8,128)}, bf16[4,8,144,512]{3,2,1,0:T(8,128)(2,1)}) custom-call(f32[4,288,128]{2,1,0:T(8,128)S(1)} %get-tuple-element.12.fresh, bf16[4,4,8,144,128]{4,3,2,1,0:T(8,128)(2,1)S(1)} %get-tuple-element.13.gathered), custom_call_target="tpu_custom_call" | custom-call | tf_op jit(solution)/shard_map/pallas_call | solution.py:566
